TPU v7x, 32 devices: a whole 2x2x4 slice. The times are simulated.
32 devices in a mesh: ctx: 8 (over y, x, core), fsdp: 4 (over z).
Axes of the slice: x: 2, y: 2, z: 4, core: 2. Of those that a mesh axis runs over, the one named last changes fastest.
Arguments:
- tokens: bfloat16 [4, 2048, 1152], P('fsdp', 'ctx'), may hold values from -6 to 6
- dealing: int32 [4, 8], P('fsdp'), may hold values from 0 to 7, each once within a row
- lengths: int32 [4, 2], P('fsdp'), may hold values from 768 to 1280, as said below
- cotangent: bfloat16 [4, 2048, 1152], P('fsdp', 'ctx'), may hold values from -6 to 6
- query_proj: bfloat16 [1152, 1024], P('fsdp'), may hold values from -0.1875 to 0.1875
- key_proj: bfloat16 [1152, 256], P('fsdp'), may hold values from -0.1875 to 0.1875
- value_proj: bfloat16 [1152, 256], P('fsdp'), may hold values from -0.1875 to 0.1875
- out_proj: bfloat16 [1024, 1152], P('fsdp'), may hold values from -0.1875 to 0.1875
- gate_proj: bfloat16 [1152, 6912], P('fsdp'), may hold values from -0.1875 to 0.1875
- up_proj: bfloat16 [1152, 6912], P('fsdp'), may hold values from -0.1875 to 0.1875
- down_proj: bfloat16 [6912, 1152], P('fsdp'), may hold values from -0.078125 to 0.078125
- gain_input: bfloat16 [1152], P('fsdp'), may hold values from 0.5 to 1.5
- gain_query: bfloat16 [256], P('fsdp'), may hold values from 1 to 2
- gain_key: bfloat16 [256], P('fsdp'), may hold values from 1 to 2
- gain_attn: bfloat16 [1152], P('fsdp'), may hold values from 0.5 to 1.5
- gain_pre: bfloat16 [1152], P('fsdp'), may hold values from 0.5 to 1.5
- gain_post: bfloat16 [1152], P('fsdp'), may hold values from 0.5 to 1.5
Outputs:
- outputs: bfloat16 [4, 2048, 1152], P('fsdp', 'ctx')
- d_tokens: float32 [4, 2048, 1152], P('fsdp', 'ctx')
- grad_query_proj: float32 [1152, 1024], P('fsdp')
- grad_key_proj: float32 [1152, 256], P('fsdp')
- grad_value_proj: float32 [1152, 256], P('fsdp')
- grad_out_proj: float32 [1024, 1152], P('fsdp')
- grad_gate_proj: float32 [1152, 6912], P('fsdp')
- grad_up_proj: float32 [1152, 6912], P('fsdp')
- grad_down_proj: float32 [6912, 1152], P('fsdp')
- grad_gain_input: float32 [1152], P('fsdp')
- grad_gain_query: float32 [256], P('fsdp')
- grad_gain_key: float32 [256], P('fsdp')
- grad_gain_attn: float32 [1152], P('fsdp')
- grad_gain_pre: float32 [1152], P('fsdp')
- grad_gain_post: float32 [1152], P('fsdp')
Inputs may be any that keep to these rules, and one draw needn't show every extreme that they name: Each row is a permutation; context index c holds the group's blocks dealing[c] and 15 - dealing[c] of 128 tokens, in that order. The two lengths of a group's sequences in order, summing to 2048; one of them is 1280, the other 768, in either order.
All inputs are finite; a program needn't handle non-finite values.
Results may differ from a plain program's by a relative error of at most 0.025.
Values may be sent and summed in bfloat16 or wider, within the bound.
A program may use at most 320 MiB of HBM per device.

v0:
```python
import jax
import jax.numpy as jnp
from jax import lax
from jax.sharding import PartitionSpec as P

EPS = 1e-06
THETA = 1000000.0


def rms_scale(values):
    return lax.rsqrt(jnp.mean(values * values, axis=-1, keepdims=True) + EPS)


def scaled(values, gain_vec):
    return values * rms_scale(values) * gain_vec


def rope_tables(positions, head_width):
    halfway = head_width // 2
    frequency = THETA ** (-(jnp.arange(halfway, dtype=jnp.float32) * 2.0 / head_width))
    angles = positions.astype(jnp.float32)[:, None] * frequency[None, :]
    return (jnp.cos(angles), jnp.sin(angles))


def rotate(values, cos_table, sin_table):
    halfway = values.shape[-1] // 2
    first_half = values[..., :halfway]
    second_half = values[..., halfway:]
    return jnp.concatenate(
        [
            first_half * cos_table - second_half * sin_table,
            second_half * cos_table + first_half * sin_table,
        ],
        axis=-1,
    )


def query_piece(raw_proj, gain_vec, cos_table, sin_table):
    head_width = gain_vec.shape[0]
    per_head = raw_proj.reshape(raw_proj.shape[0], -1, head_width)
    normed = per_head * rms_scale(per_head) * gain_vec
    return rotate(normed, cos_table[:, None, :], sin_table[:, None, :]) * head_width ** (-0.5)


def key_piece(raw_proj, gain_vec, cos_table, sin_table):
    normed = raw_proj * rms_scale(raw_proj) * gain_vec
    return rotate(normed, cos_table, sin_table)


def positions_of(dealing_row, length_row, tok_rows):
    ctx_count = dealing_row.shape[0]
    offsets = jnp.arange(tok_rows, dtype=jnp.int32)
    halves = tok_rows // 2
    blocks = jnp.where(
        offsets[None, :] < halves, dealing_row[:, None], 2 * ctx_count - 1 - dealing_row[:, None]
    )
    places = (blocks * halves + offsets[None, :] % halves).reshape(-1)
    first_len = length_row[0]
    second = places >= first_len
    in_seq = places - jnp.where(second, first_len, 0)
    return (places, second, in_seq)


def dot_last(left_side, right_side):
    return lax.dot_general(
        left_side, right_side, (((1,), (1,)), ((), ())), preferred_element_type=jnp.float32
    )


def dot_first(left_side, right_side):
    return lax.dot_general(
        left_side, right_side, (((0,), (0,)), ((), ())), preferred_element_type=jnp.float32
    )


def pair_scores(query_rows, key_rows, allowed, tok_rows):
    scores = dot_last(query_rows, key_rows).reshape(2, tok_rows, -1)
    return jnp.where(allowed[None], scores, -1e30)


def per_device(
    tokens,
    dealing,
    lengths,
    cotangent,
    query_proj,
    key_proj,
    value_proj,
    out_proj,
    gate_proj,
    up_proj,
    down_proj,
    gain_input,
    gain_query,
    gain_key,
    gain_attn,
    gain_pre,
    gain_post,
):
    attn_parts = (
        lax.all_gather(query_proj, "fsdp", axis=0, tiled=True),
        lax.all_gather(key_proj, "fsdp", axis=0, tiled=True),
        lax.all_gather(value_proj, "fsdp", axis=0, tiled=True),
        lax.all_gather(out_proj, "fsdp", axis=0, tiled=True),
        lax.all_gather(gain_input, "fsdp", axis=0, tiled=True),
        lax.all_gather(gain_query, "fsdp", axis=0, tiled=True),
        lax.all_gather(gain_key, "fsdp", axis=0, tiled=True),
        lax.all_gather(gain_attn, "fsdp", axis=0, tiled=True),
    )
    query_full, key_full, value_full, out_full = (
        attn_parts[0],
        attn_parts[1],
        attn_parts[2],
        attn_parts[3],
    )
    input_gain = attn_parts[4].astype(jnp.float32)
    query_gain = attn_parts[5].astype(jnp.float32)
    key_gain = attn_parts[6].astype(jnp.float32)
    attn_gain = attn_parts[7].astype(jnp.float32)
    mlp_parts = (
        lax.all_gather(gate_proj, "fsdp", axis=0, tiled=True),
        lax.all_gather(up_proj, "fsdp", axis=0, tiled=True),
        lax.all_gather(down_proj, "fsdp", axis=0, tiled=True),
        lax.all_gather(gain_pre, "fsdp", axis=0, tiled=True),
        lax.all_gather(gain_post, "fsdp", axis=0, tiled=True),
    )
    gate_full, up_full, down_full = (mlp_parts[0], mlp_parts[1], mlp_parts[2])
    pre_gain = mlp_parts[3].astype(jnp.float32)
    post_gain = mlp_parts[4].astype(jnp.float32)
    tok_rows = tokens.shape[1]
    head_width = query_gain.shape[0]
    places, second, in_seq = positions_of(dealing[0], lengths[0], tok_rows)
    row_start = lax.axis_index("ctx") * tok_rows
    own_place = lax.dynamic_slice_in_dim(places, row_start, tok_rows)
    own_second = lax.dynamic_slice_in_dim(second, row_start, tok_rows)
    own_seq = lax.dynamic_slice_in_dim(in_seq, row_start, tok_rows)
    allowed = (own_second[:, None] == second[None, :]) & (places[None, :] <= own_place[:, None])
    cos_table, sin_table = rope_tables(own_seq, head_width)
    inputs = tokens[0].astype(jnp.float32)
    normed_in, in_pull = jax.vjp(scaled, inputs, input_gain)
    normed_bf = normed_in.astype(jnp.bfloat16)
    query_raw = jnp.dot(normed_bf, query_full, preferred_element_type=jnp.float32)
    key_raw = jnp.dot(normed_bf, key_full, preferred_element_type=jnp.float32)
    value_raw = jnp.dot(normed_bf, value_full, preferred_element_type=jnp.float32)
    query_rot, query_pull = jax.vjp(
        lambda raw_proj, gain_vec: query_piece(raw_proj, gain_vec, cos_table, sin_table),
        query_raw,
        query_gain,
    )
    key_rot, key_pull = jax.vjp(
        lambda raw_proj, gain_vec: key_piece(raw_proj, gain_vec, cos_table, sin_table),
        key_raw,
        key_gain,
    )
    query_bf = jnp.transpose(query_rot.astype(jnp.bfloat16), (1, 0, 2))
    key_bf = key_rot.astype(jnp.bfloat16)
    value_bf = value_raw.astype(jnp.bfloat16)
    key_all, value_all = (
        lax.all_gather(key_bf, "ctx", axis=0, tiled=True),
        lax.all_gather(value_bf, "ctx", axis=0, tiled=True),
    )
    pair_count = query_bf.shape[0] // 2
    attended = []
    log_totals = []
    for pair_index in range(pair_count):
        query_rows = query_bf[2 * pair_index : 2 * pair_index + 2].reshape(2 * tok_rows, head_width)
        scores = pair_scores(query_rows, key_all, allowed, tok_rows)
        row_peak = jnp.max(scores, axis=-1, keepdims=True)
        log_total = row_peak + jnp.log(jnp.sum(jnp.exp(scores - row_peak), axis=-1, keepdims=True))
        probs_bf = jnp.exp(scores - log_total).astype(jnp.bfloat16).reshape(2 * tok_rows, -1)
        attended.append(
            jnp.dot(probs_bf, value_all, preferred_element_type=jnp.float32).reshape(
                2, tok_rows, head_width
            )
        )
        log_totals.append(log_total)
    attn_heads = jnp.concatenate(attended, axis=0)
    attn_bf = jnp.transpose(attn_heads, (1, 0, 2)).reshape(tok_rows, -1).astype(jnp.bfloat16)
    attn_proj = jnp.dot(attn_bf, out_full, preferred_element_type=jnp.float32)
    attn_normed, attn_pull = jax.vjp(scaled, attn_proj, attn_gain)
    hidden = inputs + attn_normed
    normed_mid, mid_pull = jax.vjp(scaled, hidden, pre_gain)
    mid_bf = normed_mid.astype(jnp.bfloat16)
    gate_act = jnp.dot(mid_bf, gate_full, preferred_element_type=jnp.float32)
    up_act = jnp.dot(mid_bf, up_full, preferred_element_type=jnp.float32)
    glu_value, glu_pull = jax.vjp(
        lambda gate_in, up_in: jax.nn.gelu(gate_in, approximate=True) * up_in, gate_act, up_act
    )
    glu_bf = glu_value.astype(jnp.bfloat16)
    mlp_proj = jnp.dot(glu_bf, down_full, preferred_element_type=jnp.float32)
    post_value, post_pull = jax.vjp(scaled, mlp_proj, post_gain)
    outputs_bf = (hidden + post_value).astype(jnp.bfloat16)
    d_out = cotangent[0].astype(jnp.float32)
    d_mlp, d_post_gain = post_pull(d_out)
    d_mlp_bf = d_mlp.astype(jnp.bfloat16)
    grad_down = dot_first(glu_bf, d_mlp_bf)
    d_glu = dot_last(d_mlp_bf, down_full)
    d_gate, d_up = glu_pull(d_glu)
    d_gate_bf = d_gate.astype(jnp.bfloat16)
    d_up_bf = d_up.astype(jnp.bfloat16)
    grad_gate = dot_first(mid_bf, d_gate_bf)
    grad_up = dot_first(mid_bf, d_up_bf)
    d_mid = dot_last(d_gate_bf, gate_full) + dot_last(d_up_bf, up_full)
    d_hidden_part, d_pre_gain = mid_pull(d_mid)
    d_hidden = d_out + d_hidden_part
    d_attn_proj, d_attn_gain = attn_pull(d_hidden)
    d_proj_bf = d_attn_proj.astype(jnp.bfloat16)
    grad_out = dot_first(attn_bf, d_proj_bf)
    d_attn_bf = dot_last(d_proj_bf, out_full).astype(jnp.bfloat16)
    d_attn_heads = jnp.transpose(d_attn_bf.reshape(tok_rows, -1, head_width), (1, 0, 2))
    key_back, value_back = (key_all, value_all)
    group_rows = key_back.shape[0]
    key_grad = jnp.zeros((group_rows, head_width), jnp.float32)
    value_grad = jnp.zeros((group_rows, head_width), jnp.float32)
    query_grads = []
    for pair_index in range(pair_count):
        query_rows = query_bf[2 * pair_index : 2 * pair_index + 2].reshape(2 * tok_rows, head_width)
        d_rows = d_attn_heads[2 * pair_index : 2 * pair_index + 2].reshape(2 * tok_rows, head_width)
        scores = pair_scores(query_rows, key_back, allowed, tok_rows)
        prob_full = jnp.exp(scores - log_totals[pair_index])
        d_probs = dot_last(d_rows, value_back).reshape(2, tok_rows, -1)
        inner_sum = jnp.sum(prob_full * d_probs, axis=-1, keepdims=True)
        d_scores = (
            (prob_full * (d_probs - inner_sum)).astype(jnp.bfloat16).reshape(2 * tok_rows, -1)
        )
        prob_bf = prob_full.astype(jnp.bfloat16).reshape(2 * tok_rows, -1)
        query_grads.append(
            jnp.dot(d_scores, key_back, preferred_element_type=jnp.float32).reshape(
                2, tok_rows, head_width
            )
        )
        key_grad = key_grad + dot_first(d_scores, query_rows)
        value_grad = value_grad + dot_first(prob_bf, d_rows)
    kv_terms = jnp.concatenate([key_grad, value_grad], axis=1)
    kv_own = lax.psum_scatter(
        kv_terms.astype(jnp.bfloat16), "ctx", scatter_dimension=0, tiled=True
    ).astype(jnp.float32)
    d_key = kv_own[:, :head_width]
    d_value_bf = kv_own[:, head_width:].astype(jnp.bfloat16)
    d_query = jnp.transpose(jnp.concatenate(query_grads, axis=0), (1, 0, 2))
    d_query_raw, d_query_gain = query_pull(d_query)
    d_key_raw, d_key_gain = key_pull(d_key)
    d_query_bf = d_query_raw.astype(jnp.bfloat16)
    d_key_bf = d_key_raw.astype(jnp.bfloat16)
    grad_query = dot_first(normed_bf, d_query_bf)
    grad_key = dot_first(normed_bf, d_key_bf)
    grad_value = dot_first(normed_bf, d_value_bf)
    d_normed = (
        dot_last(d_query_bf, query_full)
        + dot_last(d_key_bf, key_full)
        + dot_last(d_value_bf, value_full)
    )
    d_inputs_part, d_input_gain = in_pull(d_normed)
    d_inputs = d_hidden + d_inputs_part
    shards = (
        lax.psum_scatter(
            grad_query.astype(jnp.bfloat16), "fsdp", scatter_dimension=0, tiled=True
        ).astype(jnp.float32),
        lax.psum_scatter(
            grad_key.astype(jnp.bfloat16), "fsdp", scatter_dimension=0, tiled=True
        ).astype(jnp.float32),
        lax.psum_scatter(
            grad_value.astype(jnp.bfloat16), "fsdp", scatter_dimension=0, tiled=True
        ).astype(jnp.float32),
        lax.psum_scatter(
            grad_out.astype(jnp.bfloat16), "fsdp", scatter_dimension=0, tiled=True
        ).astype(jnp.float32),
        lax.psum_scatter(
            grad_gate.astype(jnp.bfloat16), "fsdp", scatter_dimension=0, tiled=True
        ).astype(jnp.float32),
        lax.psum_scatter(
            grad_up.astype(jnp.bfloat16), "fsdp", scatter_dimension=0, tiled=True
        ).astype(jnp.float32),
        lax.psum_scatter(
            grad_down.astype(jnp.bfloat16), "fsdp", scatter_dimension=0, tiled=True
        ).astype(jnp.float32),
        lax.psum_scatter(
            d_input_gain.astype(jnp.bfloat16), "fsdp", scatter_dimension=0, tiled=True
        ).astype(jnp.float32),
        lax.psum_scatter(
            d_query_gain.astype(jnp.bfloat16), "fsdp", scatter_dimension=0, tiled=True
        ).astype(jnp.float32),
        lax.psum_scatter(
            d_key_gain.astype(jnp.bfloat16), "fsdp", scatter_dimension=0, tiled=True
        ).astype(jnp.float32),
        lax.psum_scatter(
            d_attn_gain.astype(jnp.bfloat16), "fsdp", scatter_dimension=0, tiled=True
        ).astype(jnp.float32),
        lax.psum_scatter(
            d_pre_gain.astype(jnp.bfloat16), "fsdp", scatter_dimension=0, tiled=True
        ).astype(jnp.float32),
        lax.psum_scatter(
            d_post_gain.astype(jnp.bfloat16), "fsdp", scatter_dimension=0, tiled=True
        ).astype(jnp.float32),
    )
    summed = (
        lax.psum(shards[0].astype(jnp.bfloat16), "ctx").astype(jnp.float32),
        lax.psum(shards[1].astype(jnp.bfloat16), "ctx").astype(jnp.float32),
        lax.psum(shards[2].astype(jnp.bfloat16), "ctx").astype(jnp.float32),
        lax.psum(shards[3].astype(jnp.bfloat16), "ctx").astype(jnp.float32),
        lax.psum(shards[4].astype(jnp.bfloat16), "ctx").astype(jnp.float32),
        lax.psum(shards[5].astype(jnp.bfloat16), "ctx").astype(jnp.float32),
        lax.psum(shards[6].astype(jnp.bfloat16), "ctx").astype(jnp.float32),
        lax.psum(shards[7].astype(jnp.bfloat16), "ctx").astype(jnp.float32),
        lax.psum(shards[8].astype(jnp.bfloat16), "ctx").astype(jnp.float32),
        lax.psum(shards[9].astype(jnp.bfloat16), "ctx").astype(jnp.float32),
        lax.psum(shards[10].astype(jnp.bfloat16), "ctx").astype(jnp.float32),
        lax.psum(shards[11].astype(jnp.bfloat16), "ctx").astype(jnp.float32),
        lax.psum(shards[12].astype(jnp.bfloat16), "ctx").astype(jnp.float32),
    )
    return (
        outputs_bf[None],
        d_inputs[None],
        summed[0],
        summed[1],
        summed[2],
        summed[3],
        summed[4],
        summed[5],
        summed[6],
        summed[7],
        summed[8],
        summed[9],
        summed[10],
        summed[11],
        summed[12],
    )


def solution(mesh):
    return jax.shard_map(
        per_device,
        mesh=mesh,
        in_specs=(
            P("fsdp", "ctx", None),
            P("fsdp", None),
            P("fsdp", None),
            P("fsdp", "ctx", None),
            P("fsdp", None),
            P("fsdp", None),
            P("fsdp", None),
            P("fsdp", None),
            P("fsdp", None),
            P("fsdp", None),
            P("fsdp", None),
            P("fsdp"),
            P("fsdp"),
            P("fsdp"),
            P("fsdp"),
            P("fsdp"),
            P("fsdp"),
        ),
        out_specs=(
            P("fsdp", "ctx", None),
            P("fsdp", "ctx", None),
            P("fsdp", None),
            P("fsdp", None),
            P("fsdp", None),
            P("fsdp", None),
            P("fsdp", None),
            P("fsdp", None),
            P("fsdp", None),
            P("fsdp"),
            P("fsdp"),
            P("fsdp"),
            P("fsdp"),
            P("fsdp"),
            P("fsdp"),
        ),
        check_vma=False,
    )
```

profile of v0, /device:TPU:0, one launch (start us, length us, event | category | flops | bytes accessed | tf_op | source)
XLA Modules:
  0.0 2286.2 jit_solution(13241686103695052508)
XLA Ops:
  8.0 1.3 fusion.97
  15.8 21.8 all-reduce.19
  40.5 1.3 fusion.25
  41.7 23.0 %all_gather.48 = bf16[1152,256]{1,0:T(8,128)(2,1)S(1)} all-gather(bf16[288,256]{1,0:T(8,128)(2,1)} %param.22), channel_id=1, replica_groups=mesh['ctx'=8,'fsdp'=4] {'fsdp'}, dimensions={0}, use_global_device_ids=true | all-gather | bytes 737280 | tf_op jit(solution)/shard_map/all_gather | solution.py:102
  64.7 1.8 multiply_reduce_fusion.14
  67.3 1.3 fusion.70
  69.3 16.4 all_gather.51
  86.6 1.0 convolution_convert_fusion.10
  90.8 3.2 copy.42
  96.5 3.8 all-gather.10.cloned.1.call-done
  100.2 2.3 select_reduce_fusion.1
  102.5 2.0 exponential_reduce_fusion.1
  104.5 1.2 exponential_reduce_fusion
  106.5 19.7 all-gather.12.cloned.1.call-done
  126.2 3.8 convolution_convert_fusion.8
  130.3 1.2 convolution_convert_fusion.9
  131.6 46.6 %all-gather.14.cloned.1.call-done = bf16[1024,1152]{1,0:T(8,128)(2,1)} async-done(((bf16[256,1152]{1,0:T(8,128)(2,1)}), bf16[1024,1152]{1,0:T(8,128)(2,1)}) %all-gather.14.cloned.1.call-update) | async-done | bytes 2359312 | tf_op jit(solution)/shard_map/all_gather | solution.py:104
  178.2 2.6 multiply_reduce_fusion.8
  182.8 268.5 %all-gather.16.cloned.1.call-done = bf16[1152,6912]{1,0:T(8,128)(2,1)} async-done(((bf16[288,6912]{1,0:T(8,128)(2,1)}), bf16[1152,6912]{1,0:T(8,128)(2,1)}) %all-gather.16.cloned.1.call-update) | async-done | bytes 15925264 | tf_op jit(solution)/shard_map/all_gather | solution.py:121
  451.3 14.0 fusion.98
  465.3 258.5 %all-gather.18.cloned.1.call-done = bf16[1152,6912]{1,0:T(8,128)(2,1)} async-done(((bf16[288,6912]{1,0:T(8,128)(2,1)}), bf16[1152,6912]{1,0:T(8,128)(2,1)}) %all-gather.18.cloned.1.call-update) | async-done | bytes 15925264 | tf_op jit(solution)/shard_map/all_gather | solution.py:122
  723.8 14.4 multiply_convert_fusion.1
  738.2 258.2 %all-gather.20.cloned.1.call-done = bf16[6912,1152]{1,0:T(8,128)(2,1)} async-done(((bf16[1728,1152]{1,0:T(8,128)(2,1)}), bf16[6912,1152]{1,0:T(8,128)(2,1)}) %all-gather.20.cloned.1.call-update) | async-done | bytes 15925264 | tf_op jit(solution)/shard_map/all_gather | solution.py:123
  996.4 10.4 multiply_reduce_fusion.6
  1007.3 1.6 fusion.29
  1008.9 17.3 multiply_convert_fusion
  1026.2 12.4 fusion.99
  1038.6 13.3 multiply_reduce_fusion.2
  1051.9 2.2 multiply_reduce_fusion.3
  1054.3 1.8 copy-done.26
  1057.1 1.5 copy-done.4
  1058.5 1.4 convolution_bitcast_fusion.2
  1060.7 1.4 fusion.11
  1062.9 3.2 multiply_reduce_fusion.1
  1066.1 2.3 multiply_convert_fusion.3
  1069.9 1.5 pad_maximum_fusion
  1071.5 39.5 %reduce-scatter.9.cloned.1.call-done = bf16[256,512]{0,1:T(8,128)(2,1)} async-done(((bf16[2048,512]{0,1:T(8,128)(2,1)}), bf16[256,512]{0,1:T(8,128)(2,1)}) %reduce-scatter.9.cloned.1.call-update) | async-done | bytes 262160 | tf_op jit(solution)/shard_map/reduce_scatter | solution.py:235
  1113.6 1.3 convolution_convert_fusion.6
  1114.9 2.7 fusion.43
  1118.4 1.1 fusion.36
  1119.5 1.3 convolution_convert_fusion.5
  1120.9 1.3 multiply_add_fusion.1
  1122.8 2.3 convolution_convert_fusion.4
  1125.2 2.3 convolution_convert_fusion.3
  1127.5 9.9 convolution_convert_fusion.1
  1137.5 10.2 convolution_convert_fusion
  1147.8 1.0 copy-done.23
  1148.8 10.9 convolution_convert_fusion.2
  1159.8 49.1 %reduce-scatter.11.cloned.1.call-done = bf16[288,1024]{1,0:T(8,128)(2,1)} async-done(((bf16[1152,1024]{1,0:T(8,128)(2,1)}), bf16[288,1024]{1,0:T(8,128)(2,1)}) %reduce-scatter.11.cloned.1.call-update) | async-done | bytes 589840 | tf_op jit(solution)/shard_map/reduce_scatter | solution.py:256
  1208.9 50.4 %reduce-scatter.17.cloned.1.call-done = bf16[256,1152]{1,0:T(8,128)(2,1)} async-done(((bf16[1024,1152]{1,0:T(8,128)(2,1)}), bf16[256,1152]{1,0:T(8,128)(2,1)}) %reduce-scatter.17.cloned.1.call-update) | async-done | bytes 589840 | tf_op jit(solution)/shard_map/reduce_scatter | solution.py:265
  1259.4 269.4 %reduce-scatter.19.cloned.1.call-done = bf16[288,6912]{1,0:T(8,128)(2,1)} async-done(((bf16[1152,6912]{1,0:T(8,128)(2,1)}), bf16[288,6912]{1,0:T(8,128)(2,1)}) %reduce-scatter.19.cloned.1.call-update) | async-done | bytes 3981328 | tf_op jit(solution)/shard_map/reduce_scatter | solution.py:268
  1528.8 270.3 %reduce-scatter.21.cloned.1.call-done = bf16[288,6912]{1,0:T(8,128)(2,1)} async-done(((bf16[1152,6912]{1,0:T(8,128)(2,1)}), bf16[288,6912]{1,0:T(8,128)(2,1)}) %reduce-scatter.21.cloned.1.call-update) | async-done | bytes 3981328 | tf_op jit(solution)/shard_map/reduce_scatter | solution.py:271
  1799.1 270.4 %reduce-scatter.23.cloned.1.call-done = bf16[1728,1152]{1,0:T(8,128)(2,1)} async-done(((bf16[6912,1152]{1,0:T(8,128)(2,1)}), bf16[1728,1152]{1,0:T(8,128)(2,1)}) %reduce-scatter.23.cloned.1.call-update) | async-done | bytes 3981328 | tf_op jit(solution)/shard_map/reduce_scatter | solution.py:274
  2074.0 18.3 all-reduce.18
  2092.8 13.4 all-reduce.16
  2109.5 1.3 fusion.32
  2110.9 148.8 %all-reduce.22.cloned.1.call-done = (bf16[288,1024]{1,0:T(8,128)(2,1)}, bf16[288,256]{1,0:T(8,128)(2,1)}, bf16[288,256]{1,0:T(8,128)(2,1)}, bf16[256,1152]{1,0:T...) async-done(((bf16[288,1024]{1,0:T(8,128)(2,1)}, bf16[288,256]{1,0:T(8,128)(2,1)}, bf16[288,256]{1,0:T(8,128)(2,1)}, ...) | async-done | bytes 13418512 | tf_op jit(solution)/shard_map/psum | solution.py:297
  2259.7 2.4 convert_element_type.253
  2262.1 1.6 convert_element_type.255
  2263.7 1.6 convert_element_type.257
  2265.4 2.2 convert_element_type.259
  2267.5 4.0 convert_element_type.261
  2271.5 4.0 convert_element_type.263
  2275.5 3.8 convert_element_type.265
  (220 shorter events, 35.5 us)
Async XLA Ops:
  7.2 83.6 %all-gather.8.cloned.1.call-start = ((), (), s32[]{:S(2)}) async-start(), calls=%async_computation.8 | async-start | bytes 2949120 | tf_op jit(solution)/shard_map/all_gather | solution.py:101
  7.9 92.3 %all-gather.10.cloned.1.call-start = ((), (), s32[]{:S(2)}) async-start(), calls=%async_computation.9 | async-start | bytes 1179648 | tf_op jit(solution)/shard_map/all_gather | solution.py:159
  39.0 30.3 %copy-start.43 = (bf16[288,256]{1,0:T(8,128)(2,1)S(1)}, bf16[288,256]{1,0:T(8,128)(2,1)}, u32[]{:S(2)}) copy-start(bf16[288,256]{1,0:T(8,128)(2,1)} %param.23) | copy-start | bytes 442372
  39.0 46.8 %copy-start.53 = (f32[128]{0:T(128)}, f32[128]{0:T(128)S(1)}, u32[]{:S(2)}) copy-start(f32[128]{0:T(128)S(1)} %negate_power_fusion) | copy-start | bytes 1540
  41.7 44.1 %copy-start.44 = (f32[256]{0:T(256)}, f32[256]{0:T(256)S(1)}, u32[]{:S(2)}) copy-start(f32[256]{0:T(256)S(1)} %fusion.25) | copy-start | bytes 3076
  41.7 44.9 %copy-start.5 = (bf16[1,256,1152]{2,1,0:T(8,128)(2,1)S(1)}, bf16[1,256,1152]{2,1,0:T(8,128)(2,1)}, u32[]{:S(2)}) copy-start(bf16[1,256,1152]{2,1,0:T(8,128)(2,1)} %param.17) | copy-start | bytes 1769476
  64.7 2.6 copy-start.29
  66.5 21.7 copy-start.51
  69.3 56.9 %all-gather.12.cloned.1.call-start = ((), (), s32[]{:S(2)}) async-start(), calls=%async_computation.10 | async-start | bytes 1179648 | tf_op jit(solution)/shard_map/all_gather | solution.py:160
  87.7 90.5 %all-gather.14.cloned.1.call-start = ((), (), s32[]{:S(2)}) async-start(), calls=%async_computation.11 | async-start | bytes 2949120 | tf_op jit(solution)/shard_map/all_gather | solution.py:104
  88.3 363.0 %all-gather.16.cloned.1.call-start = ((), (), s32[]{:S(2)}) async-start(), calls=%async_computation.12 | async-start | bytes 19906560 | tf_op jit(solution)/shard_map/all_gather | solution.py:121
  88.8 634.9 %all-gather.18.cloned.1.call-start = ((), (), s32[]{:S(2)}) async-start(), calls=%async_computation.13 | async-start | bytes 19906560 | tf_op jit(solution)/shard_map/all_gather | solution.py:122
  89.4 907.0 %all-gather.20.cloned.1.call-start = ((), (), s32[]{:S(2)}) async-start(), calls=%async_computation.14 | async-start | bytes 19906560 | tf_op jit(solution)/shard_map/all_gather | solution.py:123
  90.2 1020.8 %reduce-scatter.9.cloned.1.call-start = ((), (), s32[]{:S(2)}) async-start(), calls=%async_computation.15 | async-start | bytes 2359296 | tf_op jit(solution)/shard_map/reduce_scatter | solution.py:235
  94.0 2.2 copy-start.33
  94.0 2.2 copy-start.35
  96.5 6.0 copy-start.21
  100.2 2.3 copy-start.37
  102.5 2.0 copy-start
  104.5 2.0 copy-start.3
  126.2 3.8 copy-start.1
  126.2 4.1 copy-start.16
  131.5 49.2 %copy-start.14 = (bf16[4,256,256]{1,2,0:T(8,128)(2,1)}, bf16[4,256,256]{1,2,0:T(8,128)(2,1)S(1)}, u32[]{:S(2)}) copy-start(bf16[4,256,256]{1,2,0:T(8,128)(2,1)S(1)} %pad_maximum_fusion.1) | copy-start | bytes 1572868
  180.8 2.0 copy-start.46
  996.4 10.5 copy-start.13
  1026.2 12.4 copy-start.49
  1051.9 2.2 copy-start.47
  1054.0 3.0 copy-start.6
  1054.0 2.1 copy-start.26
  1056.1 2.4 copy-start.4
  1058.5 2.2 copy-start.2
  1060.7 1.4 copy-start.17
  1066.1 2.3 copy-start.22
  1068.4 1.5 copy-start.11
  1071.4 40.6 %copy-start.54 = (f32[128]{0:T(128)S(1)}, f32[128]{0:T(128)}, u32[]{:S(2)}) copy-start(f32[128]{0:T(128)} %copy-done.53) | copy-start | bytes 1540
  1071.4 41.2 %copy-start.25 = (f32[256,256]{0,1:T(8,128)S(1)}, f32[256,256]{0,1:T(8,128)}, u32[]{:S(2)}) copy-start(f32[256,256]{0,1:T(8,128)} %copy-done.24) | copy-start | bytes 786436
  1071.4 41.4 %copy-start.52 = (f32[256]{0:T(256)S(1)}, f32[256]{0:T(256)}, u32[]{:S(2)}) copy-start(f32[256]{0:T(256)} %copy-done.51) | copy-start | bytes 3076
  1071.4 88.4 %reduce-scatter.13.cloned.1.call-start = ((), (), s32[]{:S(2)}) async-start(), calls=%async_computation.17 | async-start | bytes 737280 | tf_op jit(solution)/shard_map/reduce_scatter | solution.py:259
  1114.9 45.0 %reduce-scatter.15.cloned.1.call-start = ((), (), s32[]{:S(2)}) async-start(), calls=%async_computation.18 | async-start | bytes 737280 | tf_op jit(solution)/shard_map/reduce_scatter | solution.py:262
  1114.9 2.7 copy-start.38
  1117.6 1.9 copy-start.39
  1118.4 2.5 copy-start.34
  1118.4 2.5 copy-start.36
  1119.5 2.7 copy-start.9
  1120.8 88.1 %reduce-scatter.11.cloned.1.call-start = ((), (), s32[]{:S(2)}) async-start(), calls=%async_computation.16 | async-start | bytes 2949120 | tf_op jit(solution)/shard_map/reduce_scatter | solution.py:256
  1122.8 2.4 copy-start.15
  1122.8 2.4 copy-start.28
  1125.1 2.4 copy-start.12
  1125.1 134.2 %reduce-scatter.17.cloned.1.call-start = ((), (), s32[]{:S(2)}) async-start(), calls=%async_computation.19 | async-start | bytes 2949120 | tf_op jit(solution)/shard_map/reduce_scatter | solution.py:265
  1127.5 401.3 %reduce-scatter.19.cloned.1.call-start = ((), (), s32[]{:S(2)}) async-start(), calls=%async_computation.20 | async-start | bytes 19906560 | tf_op jit(solution)/shard_map/reduce_scatter | solution.py:268
  1137.5 661.6 %reduce-scatter.21.cloned.1.call-start = ((), (), s32[]{:S(2)}) async-start(), calls=%async_computation.21 | async-start | bytes 19906560 | tf_op jit(solution)/shard_map/reduce_scatter | solution.py:271
  1147.7 1.1 copy-start.23
  1147.8 921.7 %reduce-scatter.23.cloned.1.call-start = ((), (), s32[]{:S(2)}) async-start(), calls=%async_computation.22 | async-start | bytes 19906560 | tf_op jit(solution)/shard_map/reduce_scatter | solution.py:274
  1159.7 1100.0 %all-reduce.22.cloned.1.call-start = ((), (), s32[]{:S(2)}) async-start(), calls=%async_computation.23 | async-start | bytes 26836992 | tf_op jit(solution)/shard_map/psum | solution.py:297
  2069.5 1.7 copy-start.10
  2071.1 1.1 copy-start.30
  2071.1 1.1 copy-start.42
  2072.2 1.1 copy-start.32
  2072.2 1.1 copy-start.40
  2073.3 36.2 %copy-start.45 = (f32[256]{0:T(256)S(1)}, f32[256]{0:T(256)}, u32[]{:S(2)}) copy-start(f32[256]{0:T(256)} %copy-done.44) | copy-start | bytes 3076
  2073.3 36.2 %copy-start.7 = (f32[256,1152]{1,0:T(8,128)S(1)}, f32[256,1152]{1,0:T(8,128)}, u32[]{:S(2)}) copy-start(f32[256,1152]{1,0:T(8,128)} %copy-done.6) | copy-start | bytes 3538948
  2259.7 7.8 copy-start.20
  2267.5 4.0 copy-start.19
  2271.5 4.0 copy-start.18
  (7 other events, 5.3 us)
Sparse Core Ops, SparseCore 0:
  9.6 66.3 all-gather.7
  78.5 21.7 all-gather.9
  102.7 23.4 all-gather.11
  127.6 50.4 all-gather.13
  179.6 271.6 all-gather.15
  452.7 271.0 all-gather.17
  725.3 271.0 all-gather.19
  1071.6 39.4 reduce-scatter.8
  1115.0 21.9 reduce-scatter.12
  1139.2 20.2 reduce-scatter.14
  1162.5 46.3 reduce-scatter.10
  1211.8 47.5 reduce-scatter.16
  1261.8 266.8 reduce-scatter.18
  1531.0 268.0 reduce-scatter.20
  1801.4 268.0 reduce-scatter.22
  2074.2 185.4 all-reduce.21
where the time goes:
time: 2290 us
  waiting for transfers between devices  1960 us (86%)
  matrix products  150 us (7%)
  blocking collectives  92.9 us (4%)
  other arithmetic  46.9 us (2%)
    reduce_scatter x1, waiting for transfers between devices, per_device(): lax.psum_scatter(grad_down.astype(jnp.bfloat16), 'fsdp', scatter_dimensio...  270 us
    reduce_scatter x1, waiting for transfers between devices, per_device(): lax.psum_scatter(grad_up.astype(jnp.bfloat16), 'fsdp', scatter_dimension=...  270 us
    reduce_scatter x1, waiting for transfers between devices, per_device(): lax.psum_scatter(grad_gate.astype(jnp.bfloat16), 'fsdp', scatter_dimensio...  269 us
    all_gather x1, waiting for transfers between devices, per_device(): lax.all_gather(gate_proj, 'fsdp', axis=0, tiled=True)  269 us
    all_gather x1, waiting for transfers between devices, per_device(): lax.all_gather(up_proj, 'fsdp', axis=0, tiled=True)  258 us
    all_gather x1, waiting for transfers between devices, per_device(): lax.all_gather(down_proj, 'fsdp', axis=0, tiled=True)  258 us
    psum x1, waiting for transfers between devices, per_device(): lax.psum(shards[0].astype(jnp.bfloat16), 'ctx').astype(jnp.float32)  149 us
    dot_general x11, matrix products, dot_last(): lax.dot_general(left_side, right_side, (((1,), (1,)), ((), ())), preferre...  53.9 us
  transfers between devices with their start and end apart: 16, of which 13 were waited for; matrix products, arithmetic and copies ran while one was open for 5% of the time, Pallas kernels for 0%

commit v1 on v0

v1 whole, which is shorter than its diff:
```python
import jax
import jax.numpy as jnp
from jax import lax
from jax.sharding import PartitionSpec as P

EPS = 1e-06
THETA = 1000000.0


def rms_scale(values):
    return lax.rsqrt(jnp.mean(values * values, axis=-1, keepdims=True) + EPS)


def scaled(values, gain_vec):
    return values * rms_scale(values) * gain_vec


def rope_tables(positions, head_width):
    halfway = head_width // 2
    frequency = THETA ** (-(jnp.arange(halfway, dtype=jnp.float32) * 2.0 / head_width))
    angles = positions.astype(jnp.float32)[:, None] * frequency[None, :]
    return (jnp.cos(angles), jnp.sin(angles))


def rotate(values, cos_table, sin_table):
    halfway = values.shape[-1] // 2
    first_half = values[..., :halfway]
    second_half = values[..., halfway:]
    return jnp.concatenate(
        [
            first_half * cos_table - second_half * sin_table,
            second_half * cos_table + first_half * sin_table,
        ],
        axis=-1,
    )


def query_piece(raw_proj, gain_vec, cos_table, sin_table):
    head_width = gain_vec.shape[0]
    per_head = raw_proj.reshape(raw_proj.shape[0], -1, head_width)
    normed = per_head * rms_scale(per_head) * gain_vec
    return rotate(normed, cos_table[:, None, :], sin_table[:, None, :]) * head_width ** (-0.5)


def key_piece(raw_proj, gain_vec, cos_table, sin_table):
    normed = raw_proj * rms_scale(raw_proj) * gain_vec
    return rotate(normed, cos_table, sin_table)


def positions_of(dealing_row, length_row, tok_rows):
    ctx_count = dealing_row.shape[0]
    offsets = jnp.arange(tok_rows, dtype=jnp.int32)
    halves = tok_rows // 2
    blocks = jnp.where(
        offsets[None, :] < halves, dealing_row[:, None], 2 * ctx_count - 1 - dealing_row[:, None]
    )
    places = (blocks * halves + offsets[None, :] % halves).reshape(-1)
    first_len = length_row[0]
    second = places >= first_len
    in_seq = places - jnp.where(second, first_len, 0)
    return (places, second, in_seq)


def dot_last(left_side, right_side):
    return lax.dot_general(
        left_side, right_side, (((1,), (1,)), ((), ())), preferred_element_type=jnp.float32
    )


def dot_first(left_side, right_side):
    return lax.dot_general(
        left_side, right_side, (((0,), (0,)), ((), ())), preferred_element_type=jnp.float32
    )


def per_device(
    tokens,
    dealing,
    lengths,
    cotangent,
    query_proj,
    key_proj,
    value_proj,
    out_proj,
    gate_proj,
    up_proj,
    down_proj,
    gain_input,
    gain_query,
    gain_key,
    gain_attn,
    gain_pre,
    gain_post,
):
    ctx_count = dealing.shape[1]
    fsdp_count = lax.axis_size("fsdp")
    ctx_index = lax.axis_index("ctx")
    tok_rows, width = tokens.shape[1], tokens.shape[2]
    head_cols = query_proj.shape[1]
    head_width = key_proj.shape[1]
    qkv_cols = head_cols + 2 * head_width

    qkv_own = jnp.concatenate([query_proj, key_proj, value_proj], axis=1)
    qkv_piece = qkv_own.shape[0] // ctx_count
    gains_own = jnp.concatenate(
        [gain_input, gain_query, gain_key, gain_attn, gain_pre, gain_post]
    )
    gain_sizes = [
        v.shape[0] for v in (gain_input, gain_query, gain_key, gain_attn, gain_pre, gain_post)
    ]
    gain_row = jnp.pad(gains_own, (0, qkv_cols - gains_own.shape[0]))[None]
    qkv_send = jnp.concatenate(
        [lax.dynamic_slice_in_dim(qkv_own, ctx_index * qkv_piece, qkv_piece), gain_row], axis=0
    )
    qkv_got = lax.all_gather(qkv_send, ("fsdp", "ctx"), axis=0).reshape(
        fsdp_count, ctx_count, qkv_piece + 1, qkv_cols
    )
    qkv_full = qkv_got[:, :, :qkv_piece].reshape(-1, qkv_cols)
    gains_got = qkv_got[:, 0, qkv_piece].astype(jnp.float32)
    gain_full = []
    at = 0
    for size in gain_sizes:
        gain_full.append(gains_got[:, at : at + size].reshape(-1))
        at += size
    input_gain, query_gain, key_gain, attn_gain, pre_gain, post_gain = gain_full
    out_piece = out_proj.shape[0] // ctx_count
    out_full = lax.all_gather(
        lax.dynamic_slice_in_dim(out_proj, ctx_index * out_piece, out_piece),
        ("fsdp", "ctx"),
        axis=0,
        tiled=True,
    )

    unit_rows = down_proj.shape[0]
    unit_piece = unit_rows // ctx_count
    unit_own = fsdp_count * unit_piece
    unit_pad = -(-unit_own // 128) * 128

    def unit_columns(weight):
        parts = [
            lax.dynamic_slice_in_dim(
                weight, index * unit_rows + ctx_index * unit_piece, unit_piece, axis=1
            )
            for index in range(fsdp_count)
        ]
        parts.append(jnp.zeros((weight.shape[0], unit_pad - unit_own), weight.dtype))
        return jnp.concatenate(parts, axis=1)

    gate_up = lax.all_gather(
        jnp.concatenate([unit_columns(gate_proj), unit_columns(up_proj)], axis=1),
        "fsdp",
        axis=0,
        tiled=True,
    )
    down_own = lax.all_gather(
        lax.dynamic_slice_in_dim(down_proj, ctx_index * unit_piece, unit_piece),
        "fsdp",
        axis=0,
        tiled=True,
    )
    down_own = jnp.pad(down_own, ((0, unit_pad - unit_own), (0, 0)))

    places, second, in_seq = positions_of(dealing[0], lengths[0], tok_rows)
    row_start = ctx_index * tok_rows
    own_place = lax.dynamic_slice_in_dim(places, row_start, tok_rows)
    own_second = lax.dynamic_slice_in_dim(second, row_start, tok_rows)
    own_seq = lax.dynamic_slice_in_dim(in_seq, row_start, tok_rows)
    allowed = (own_second[:, None] == second[None, :]) & (places[None, :] <= own_place[:, None])
    cos_table, sin_table = rope_tables(own_seq, head_width)
    inputs = tokens[0].astype(jnp.float32)
    normed_in, in_pull = jax.vjp(scaled, inputs, input_gain)
    normed_bf = normed_in.astype(jnp.bfloat16)
    qkv_raw = jnp.dot(normed_bf, qkv_full, preferred_element_type=jnp.float32)
    query_raw = qkv_raw[:, :head_cols]
    key_raw = qkv_raw[:, head_cols : head_cols + head_width]
    value_raw = qkv_raw[:, head_cols + head_width :]
    query_rot, query_pull = jax.vjp(
        lambda raw_proj, gain_vec: query_piece(raw_proj, gain_vec, cos_table, sin_table),
        query_raw,
        query_gain,
    )
    key_rot, key_pull = jax.vjp(
        lambda raw_proj, gain_vec: key_piece(raw_proj, gain_vec, cos_table, sin_table),
        key_raw,
        key_gain,
    )
    query_rows = jnp.transpose(query_rot.astype(jnp.bfloat16), (1, 0, 2)).reshape(-1, head_width)
    kv_all = lax.all_gather(
        jnp.concatenate([key_rot, value_raw], axis=1).astype(jnp.bfloat16),
        "ctx",
        axis=0,
        tiled=True,
    )
    key_all, value_all = kv_all[:, :head_width], kv_all[:, head_width:]
    heads = head_cols // head_width
    scores = dot_last(query_rows, key_all).reshape(heads, tok_rows, -1)
    weights = jnp.where(allowed[None], jnp.exp(scores), 0.0)
    totals = jnp.sum(weights, axis=-1, keepdims=True)
    probs_bf = (weights * (1.0 / totals)).astype(jnp.bfloat16).reshape(heads * tok_rows, -1)
    attn_heads = jnp.dot(probs_bf, value_all, preferred_element_type=jnp.float32).reshape(
        heads, tok_rows, head_width
    )
    attn_bf = jnp.transpose(attn_heads, (1, 0, 2)).reshape(tok_rows, -1).astype(jnp.bfloat16)
    attn_proj = jnp.dot(attn_bf, out_full, preferred_element_type=jnp.float32)
    attn_normed, attn_pull = jax.vjp(scaled, attn_proj, attn_gain)
    hidden = inputs + attn_normed
    normed_mid, mid_pull = jax.vjp(scaled, hidden, pre_gain)
    mid_all = lax.all_gather(normed_mid.astype(jnp.bfloat16), "ctx", axis=0, tiled=True)
    gate_up_act = jnp.dot(mid_all, gate_up, preferred_element_type=jnp.float32)
    gate_act, up_act = gate_up_act[:, :unit_pad], gate_up_act[:, unit_pad:]
    glu_value, glu_pull = jax.vjp(
        lambda gate_in, up_in: jax.nn.gelu(gate_in, approximate=True) * up_in, gate_act, up_act
    )
    glu_bf = glu_value.astype(jnp.bfloat16)
    mlp_part = jnp.dot(glu_bf, down_own, preferred_element_type=jnp.float32)
    mlp_proj = lax.psum_scatter(
        mlp_part.astype(jnp.bfloat16), "ctx", scatter_dimension=0, tiled=True
    ).astype(jnp.float32)
    post_value, post_pull = jax.vjp(scaled, mlp_proj, post_gain)
    outputs_bf = (hidden + post_value).astype(jnp.bfloat16)
    d_out = cotangent[0].astype(jnp.float32)
    d_mlp, d_post_gain = post_pull(d_out)
    d_mlp_all = lax.all_gather(d_mlp.astype(jnp.bfloat16), "ctx", axis=0, tiled=True)
    d_glu = dot_last(d_mlp_all, down_own)
    d_gate, d_up = glu_pull(d_glu)
    d_gate_up = jnp.concatenate([d_gate, d_up], axis=1).astype(jnp.bfloat16)
    d_mid_part = dot_last(d_gate_up, gate_up)
    d_mid = lax.psum_scatter(
        d_mid_part.astype(jnp.bfloat16), "ctx", scatter_dimension=0, tiled=True
    ).astype(jnp.float32)
    grad_down = dot_first(glu_bf, d_mlp_all)[:unit_own].astype(jnp.bfloat16)
    grad_gate_up = dot_first(mid_all, d_gate_up).astype(jnp.bfloat16)
    grad_down = lax.psum_scatter(grad_down, "fsdp", scatter_dimension=0, tiled=True)
    grad_gate_up = lax.psum_scatter(grad_gate_up, "fsdp", scatter_dimension=0, tiled=True)
    grad_down = lax.all_gather(grad_down, "ctx", axis=0, tiled=True).astype(jnp.float32)
    grad_gate_up = lax.all_gather(grad_gate_up, "ctx", axis=0)

    def unit_order(pieces):
        rows = pieces.shape[1]
        pieces = pieces.reshape(ctx_count, rows, fsdp_count, unit_piece)
        return jnp.transpose(pieces, (1, 2, 0, 3)).reshape(rows, -1).astype(jnp.float32)

    grad_gate = unit_order(grad_gate_up[:, :, :unit_own])
    grad_up = unit_order(grad_gate_up[:, :, unit_pad : unit_pad + unit_own])
    d_hidden_part, d_pre_gain = mid_pull(d_mid)
    d_hidden = d_out + d_hidden_part
    d_attn_proj, d_attn_gain = attn_pull(d_hidden)
    d_proj_bf = d_attn_proj.astype(jnp.bfloat16)
    grad_out = lax.psum_scatter(
        dot_first(attn_bf, d_proj_bf).astype(jnp.bfloat16),
        ("fsdp", "ctx"),
        scatter_dimension=0,
        tiled=True,
    )
    grad_out = lax.all_gather(grad_out, "ctx", axis=0, tiled=True).astype(jnp.float32)
    d_attn_bf = dot_last(d_proj_bf, out_full).astype(jnp.bfloat16)
    d_rows = jnp.transpose(d_attn_bf.reshape(tok_rows, -1, head_width), (1, 0, 2)).reshape(
        -1, head_width
    )
    d_probs = dot_last(d_rows, value_all)
    probs = probs_bf.astype(jnp.float32)
    inner_sum = jnp.sum(probs * d_probs, axis=-1, keepdims=True)
    d_scores = (probs * (d_probs - inner_sum)).astype(jnp.bfloat16)
    key_grad = dot_first(d_scores, query_rows)
    value_grad = dot_first(probs_bf, d_rows)
    kv_own = lax.psum_scatter(
        jnp.concatenate([key_grad, value_grad], axis=1).astype(jnp.bfloat16),
        "ctx",
        scatter_dimension=0,
        tiled=True,
    ).astype(jnp.float32)
    d_query = jnp.transpose(
        jnp.dot(d_scores, key_all, preferred_element_type=jnp.float32).reshape(
            heads, tok_rows, head_width
        ),
        (1, 0, 2),
    )
    d_query_raw, d_query_gain = query_pull(d_query)
    d_key_raw, d_key_gain = key_pull(kv_own[:, :head_width])
    d_qkv_bf = jnp.concatenate([d_query_raw, d_key_raw, kv_own[:, head_width:]], axis=1).astype(
        jnp.bfloat16
    )
    d_normed = dot_last(d_qkv_bf, qkv_full)
    d_inputs_part, d_input_gain = in_pull(d_normed)
    d_inputs = d_hidden + d_inputs_part
    grad_qkv = dot_first(normed_bf, d_qkv_bf).astype(jnp.bfloat16)
    gain_grads = jnp.concatenate(
        [
            v.reshape(fsdp_count, -1)
            for v in (
                d_input_gain,
                d_query_gain,
                d_key_gain,
                d_attn_gain,
                d_pre_gain,
                d_post_gain,
            )
        ],
        axis=1,
    ).astype(jnp.bfloat16)
    gain_grads = jnp.pad(gain_grads, ((0, 0), (0, qkv_cols - gain_grads.shape[1])))
    qkv_terms = jnp.concatenate(
        [
            grad_qkv.reshape(fsdp_count, ctx_count, qkv_piece, qkv_cols),
            jnp.broadcast_to(
                gain_grads[:, None, None], (fsdp_count, ctx_count, 1, qkv_cols)
            ),
        ],
        axis=2,
    ).reshape(fsdp_count * ctx_count, qkv_piece + 1, qkv_cols)
    qkv_sum = lax.psum_scatter(qkv_terms, ("fsdp", "ctx"), scatter_dimension=0, tiled=True)[0]
    gain_sum = qkv_sum[qkv_piece].astype(jnp.float32)
    grad_qkv = lax.all_gather(qkv_sum[:qkv_piece], "ctx", axis=0, tiled=True).astype(jnp.float32)
    gain_out = []
    at = 0
    for size in gain_sizes:
        gain_out.append(gain_sum[at : at + size])
        at += size
    return (
        outputs_bf[None],
        d_inputs[None],
        grad_qkv[:, :head_cols],
        grad_qkv[:, head_cols : head_cols + head_width],
        grad_qkv[:, head_cols + head_width :],
        grad_out,
        grad_gate,
        grad_up,
        grad_down,
        *gain_out,
    )


def solution(mesh):
    return jax.shard_map(
        per_device,
        mesh=mesh,
        in_specs=(
            P("fsdp", "ctx", None),
            P("fsdp", None),
            P("fsdp", None),
            P("fsdp", "ctx", None),
            P("fsdp", None),
            P("fsdp", None),
            P("fsdp", None),
            P("fsdp", None),
            P("fsdp", None),
            P("fsdp", None),
            P("fsdp", None),
            P("fsdp"),
            P("fsdp"),
            P("fsdp"),
            P("fsdp"),
            P("fsdp"),
            P("fsdp"),
        ),
        out_specs=(
            P("fsdp", "ctx", None),
            P("fsdp", "ctx", None),
            P("fsdp", None),
            P("fsdp", None),
            P("fsdp", None),
            P("fsdp", None),
            P("fsdp", None),
            P("fsdp", None),
            P("fsdp", None),
            P("fsdp"),
            P("fsdp"),
            P("fsdp"),
            P("fsdp"),
            P("fsdp"),
            P("fsdp"),
        ),
        check_vma=False,
    )
```

time: 2290 us -> 1110 us (0.48)
  waiting for transfers between devices: 1960 us -> 760 us
  local copies, waits for them, and re-layouts: 21.3 us -> 127 us
  blocking collectives: 92.9 us -> 27.8 us
  matrix products: 150 us -> 103 us
    reduce_scatter x8 -> x6, waiting for transfers between devices: 949 us -> 399 us  [the longest x1 105 us: per_device(): lax.psum_scatter(qkv_terms, ('fsdp', 'ctx'), scatter_dimension=0, tiled=T...]
    all_gather x7 -> x9, waiting for transfers between devices: 855 us -> 357 us  [the longest x1 74.2 us: per_device(): lax.all_gather(jnp.concatenate([unit_columns(gate_proj), unit_columns(up_...]
    psum x1 -> x0, waiting for transfers between devices: 149 us -> none  [per_device(): lax.psum(shards[0].astype(jnp.bfloat16), 'ctx').astype(jnp.float32)]
    convert_element_type x0 -> x6, local copies, waits for them, and re-layouts: none -> 72.8 us  [unit_order(): jnp.transpose(pieces, (1, 2, 0, 3)).reshape(rows, -1).astype(jnp.float32)]
    unnamed x2 -> x0, blocking collectives: 40.1 us -> none
    dot_general x11 -> x6, matrix products: 53.9 us -> 36.1 us  [dot_last(): lax.dot_general(left_side, right_side, (((1,), (1,)), ((), ())), preferre...]
    dot_general x8 -> x4, matrix products: 46.1 us -> 29.6 us  [the longest x1 13.3 us: per_device(): gate_up_act = jnp.dot(mid_all, gate_up, preferred_element_type=jnp.float32)]
  transfers between devices with their start and end apart: 16 -> 16, of which waited for: 13 -> 16; matrix products, arithmetic and copies ran while one was open for 5% -> 12% of each run, Pallas kernels for 0% -> 0%
where the time goes in v1:
time: 1110 us; the launch traced here: 1100 us
  waiting for transfers between devices  760 us (68%)
  local copies, waits for them, and re-layouts  127 us (11%)
  matrix products  103 us (9%)
  other arithmetic  66 us (6%)
  blocking collectives  27.8 us (3%)
  between operations  15.2 us (1%)
    reduce_scatter x1, waiting for transfers between devices, per_device(): lax.psum_scatter(qkv_terms, ('fsdp', 'ctx'), scatter_dimension=0, tiled=T...  105 us
    reduce_scatter x1, waiting for transfers between devices, per_device(): lax.psum_scatter(dot_first(attn_bf, d_proj_bf).astype(jnp.bfloat16), ('fs...  105 us
    all_gather x1, waiting for transfers between devices, per_device(): lax.all_gather(jnp.concatenate([unit_columns(gate_proj), unit_columns(up_...  74.2 us
    convert_element_type x6, local copies, waits for them, and re-layouts, unit_order(): jnp.transpose(pieces, (1, 2, 0, 3)).reshape(rows, -1).astype(jnp.float32)  72.8 us
    all_gather x1, waiting for transfers between devices, per_device(): lax.all_gather(qkv_send, ('fsdp', 'ctx'), axis=0)  58.2 us
    reduce_scatter x1, waiting for transfers between devices, per_device(): lax.psum_scatter(grad_gate_up, 'fsdp', scatter_dimension=0, tiled=True)  55.9 us
    all_gather x1, waiting for transfers between devices, per_device(): lax.all_gather(lax.dynamic_slice_in_dim(out_proj, ctx_index * out_piece,...  52.6 us
    reduce_scatter x1, waiting for transfers between devices, per_device(): lax.psum_scatter(mlp_part.astype(jnp.bfloat16), 'ctx', scatter_dimension=...  51.4 us
  transfers between devices with their start and end apart: 16, of which 16 were waited for; matrix products, arithmetic and copies ran while one was open for 12% of the time, Pallas kernels for 0%

profile of v1, /device:TPU:0, one launch (start us, length us, event | category | flops | bytes accessed | tf_op | source)
XLA Modules:
  0.0 1101.6 jit_solution(8603756927631348178)
XLA Ops:
  7.2 4.2 concatenate.42
  19.0 58.2 %all-gather.30.cloned.1.call-done = bf16[32,37,1536]{2,1,0:T(8,128)(2,1)} async-done(((bf16[1,37,1536]{2,1,0:T(8,128)(2,1)}), bf16[32,37,1536]{2,1,0:T(8,128)(2,1)}) %all-gather.30.cloned.1.call-update) | async-done | bytes 3637264 | tf_op jit(solution)/shard_map/all_gather | solution.py:115
  79.5 5.7 reshape.458
  85.3 3.2 fusion.55
  92.8 2.7 constant_dynamic-slice_fusion
  95.5 2.8 concatenate.46
  104.9 13.8 %all-gather.14.cloned.1.call-done = bf16[2048,512]{1,0:T(8,128)(2,1)} async-done(((bf16[256,512]{1,0:T(8,128)(2,1)}), bf16[2048,512]{1,0:T(8,128)(2,1)}) %all-gather.14.cloned.1.call-update) | async-done | bytes 2097168 | tf_op jit(solution)/shard_map/all_gather | solution.py:188
  118.7 3.3 fusion.2
  122.0 1.5 multiply_convert_fusion
  123.5 2.0 copy-done.2
  125.5 1.3 convolution_convert_fusion.7
  126.8 52.6 %all-gather.16.cloned.1.call-done = bf16[1024,1152]{1,0:T(8,128)(2,1)} async-done(((bf16[32,1152]{1,0:T(8,128)(2,1)}), bf16[1024,1152]{1,0:T(8,128)(2,1)}) %all-gather.16.cloned.1.call-update) | async-done | bytes 2359312 | tf_op jit(solution)/shard_map/all_gather | solution.py:127
  179.4 2.6 multiply_reduce_fusion.3
  183.7 1.9 constant_dynamic-slice_fusion.9
  185.9 74.2 %all-gather.20.cloned.1.call-done = bf16[1152,1792]{1,0:T(8,128)(2,1)} async-done(((bf16[288,1792]{1,0:T(8,128)(2,1)}), bf16[1152,1792]{1,0:T(8,128)(2,1)}) %all-gather.20.cloned.1.call-update) | async-done | bytes 4128784 | tf_op jit(solution)/shard_map/all_gather | solution.py:149
  260.0 39.8 %all-gather.18.cloned.1.call-done = bf16[2048,1152]{1,0:T(8,128)(2,1)} async-done(((bf16[256,1152]{1,0:T(8,128)(2,1)}), bf16[2048,1152]{1,0:T(8,128)(2,1)}) %all-gather.18.cloned.1.call-update) | async-done | bytes 4718608 | tf_op jit(solution)/shard_map/all_gather | solution.py:208
  299.8 13.3 %fusion.99 = f32[2048,1792]{0,1:T(8,128)S(1)} fusion(bf16[2048,1152]{1,0:T(8,128)(2,1)} %all-gather.18.cloned.1.call-done, bf16[1152,1792]{1,0:T(8,128)(2,1)} %all-gather.20.cloned.1.call-done), kind=kOutput, calls=%fused_computation.213 | convolution fusion | flops 8455716864 | bytes 23527424 | tf_op jit(solution)/shard_map/dot_general | solution.py:209
  313.1 5.2 copy-done.6
  318.4 3.8 multiply_convert_fusion.2
  322.1 23.7 %all-gather.22.cloned.1.call-done = bf16[864,1152]{1,0:T(8,128)(2,1)} async-done(((bf16[216,1152]{1,0:T(8,128)(2,1)}), bf16[864,1152]{1,0:T(8,128)(2,1)}) %all-gather.22.cloned.1.call-update) | async-done | bytes 1990672 | tf_op jit(solution)/shard_map/all_gather | solution.py:155
  345.8 9.3 convolution_convert_fusion
  355.2 1.4 mul.616
  356.6 51.4 %reduce-scatter.10.cloned.1.call-done = bf16[256,1152]{1,0:T(8,128)(2,1)} async-done(((bf16[2048,1152]{1,0:T(8,128)(2,1)}), bf16[256,1152]{1,0:T(8,128)(2,1)}) %reduce-scatter.10.cloned.1.call-update) | async-done | bytes 589840 | tf_op jit(solution)/shard_map/reduce_scatter | solution.py:216
  409.3 2.2 fusion.39
  411.5 2.2 fusion.35
  414.1 38.6 %all-gather.24.cloned.1.call-done = bf16[2048,1152]{1,0:T(8,128)(2,1)} async-done(((bf16[256,1152]{1,0:T(8,128)(2,1)}), bf16[2048,1152]{1,0:T(8,128)(2,1)}) %all-gather.24.cloned.1.call-update) | async-done | bytes 4718608 | tf_op jit(solution)/shard_map/all_gather | solution.py:223
  452.8 15.2 %fusion.9 = (bf16[2048,896]{0,1:T(8,128)(2,1)S(1)}, bf16[2048,896]{0,1:T(8,128)(2,1)S(1)}) fusion(f32[2048,1792]{0,1:T(8,128)} %copy-done.6, bf16[2048,1152]{1,0:T(8,128)(2,1)} %all-gather.24.cloned.1.call-done, bf16[864,1152]{1,0:T(8,128)(2,1)} %all-gather.22.cloned.1.call-done), kind=kOutput, calls=%fused_computation.21 | convolution fusion | flops 4271898624 | bytes 28729344 | tf_op jit(solution)/shard_map/dot_general | solution.py:65
  468.0 1.8 copy-done.60
  470.9 11.4 %convolution_convert_fusion.2 = bf16[2048,1152]{1,0:T(8,128)(2,1)} fusion(bf16[1152,1792]{1,0:T(8,128)(2,1)S(1)} %copy-done.59, bf16[2048,896]{0,1:T(8,128)(2,1)S(1)} %get-tuple-element.38, bf16[2048,896]{0,1:T(8,128)(2,1)S(1)} %get-tuple-element.37), kind=kOutput, calls=%fused_computation.12 | convolution fusion | flops 8472756224 | bytes 16187392 | tf_op jit(solution)/shard_map/dot_general | solution.py:65
  482.5 8.3 fusion.100
  490.9 1.5 slice.260
  492.5 43.9 %reduce-scatter.12.cloned.1.call-done = bf16[256,1152]{1,0:T(8,128)(2,1)} async-done(((bf16[2048,1152]{1,0:T(8,128)(2,1)}), bf16[256,1152]{1,0:T(8,128)(2,1)}) %reduce-scatter.12.cloned.1.call-update) | async-done | bytes 589840 | tf_op jit(solution)/shard_map/reduce_scatter | solution.py:228
  536.3 2.0 fusion.30
  539.1 3.7 multiply_reduce_fusion
  546.6 1.4 fusion
  548.0 3.0 fusion.1
  551.0 3.6 convolution_convert_fusion.5
  554.6 1.3 fusion.10
  556.0 1.5 pad_maximum_fusion.4
  557.7 15.1 %convolution_convert_fusion.3 = bf16[1152,1792]{1,0:T(8,128)(2,1)} fusion(bf16[2048,1152]{1,0:T(8,128)(2,1)} %all-gather.18.cloned.1.call-done, bf16[2048,896]{0,1:T(8,128)(2,1)} %copy-done.61, bf16[2048,896]{0,1:T(8,128)(2,1)} %copy-done.60), kind=kOutput, calls=%fused_computation.13 | convolution fusion | flops 8472461312 | bytes 16187392 | tf_op jit(solution)/shard_map/dot_general | solution.py:71
  573.9 2.2 convolution_convert_fusion.4
  576.3 4.1 reduce-scatter.22.cloned.1.call-done
  581.1 3.8 convolution_multiply_fusion
  586.4 38.8 %reduce-scatter.14.cloned.1.call-done = bf16[256,512]{1,0:T(8,128)(2,1)} async-done(((bf16[2048,512]{1,0:T(8,128)(2,1)}), bf16[256,512]{1,0:T(8,128)(2,1)}) %reduce-scatter.14.cloned.1.call-update) | async-done | bytes 262160 | tf_op jit(solution)/shard_map/reduce_scatter | solution.py:266
  630.1 4.0 fusion.28
  634.6 3.0 convolution_convert_fusion.1
  637.6 5.6 concatenate.50
  643.3 4.6 pad_maximum_fusion.3
  647.9 55.9 %reduce-scatter.20.cloned.1.call-done = bf16[288,1792]{1,0:T(8,128)(2,1)} async-done(((bf16[1152,1792]{1,0:T(8,128)(2,1)}), bf16[288,1792]{1,0:T(8,128)(2,1)}) %reduce-scatter.20.cloned.1.call-update) | async-done | bytes 1032208 | tf_op jit(solution)/shard_map/reduce_scatter | solution.py:234
  703.8 104.7 %reduce-scatter.18.cloned.1.call-done = bf16[32,1152]{1,0:T(8,128)(2,1)} async-done(((bf16[1024,1152]{1,0:T(8,128)(2,1)}), bf16[32,1152]{1,0:T(8,128)(2,1)}) %reduce-scatter.18.cloned.1.call-update) | async-done | bytes 73744 | tf_op jit(solution)/shard_map/reduce_scatter | solution.py:249
  808.5 10.1 all_gather.48
  820.5 1.3 fusion.38
  821.8 23.5 %all-gather.26.cloned.1.call-done = bf16[1728,1152]{1,0:T(8,128)(2,1)} async-done(((bf16[216,1152]{1,0:T(8,128)(2,1)}), bf16[1728,1152]{1,0:T(8,128)(2,1)}) %all-gather.26.cloned.1.call-update) | async-done | bytes 3981328 | tf_op jit(solution)/shard_map/all_gather | solution.py:235
  845.3 5.9 convert_element_type.190
  851.2 104.8 %reduce-scatter.16.cloned.1.call-done = bf16[1,37,1536]{2,1,0:T(8,128)(2,1)} async-done(((bf16[32,37,1536]{2,1,0:T(8,128)(2,1)}), bf16[1,37,1536]{2,1,0:T(8,128)(2,1)}) %reduce-scatter.16.cloned.1.call-update) | async-done | bytes 113680 | tf_op jit(solution)/shard_map/reduce_scatter | solution.py:311
  957.1 17.7 %all-gather.1 = bf16[1,288,1536]{2,0,1:T(2,128)(2,1)S(1)} all-gather(bf16[1,36,1536]{2,0,1:T(2,128)(2,1)S(1)} %copy.104), channel_id=3, replica_groups=mesh['ctx'=8,'fsdp'=4] {'ctx'}, dimensions={1}, use_global_device_ids=true | all-gather | bytes 995328 | tf_op jit(solution)/shard_map/all_gather | solution.py:313
  978.9 32.2 %all-gather.28.cloned.1.call-done = bf16[2304,1792]{1,0:T(8,128)(2,1)} async-done(((bf16[288,1792]{1,0:T(8,128)(2,1)}), bf16[2304,1792]{1,0:T(8,128)(2,1)}) %all-gather.28.cloned.1.call-update) | async-done | bytes 8257552 | tf_op jit(solution)/shard_map/all_gather | solution.py:236
  1011.1 11.0 slice_convert_fusion
  1022.1 12.7 %reshape.477 = f32[8,288,4,216]{3,2,1,0:T(4,128)} reshape(f32[8,288,864]{2,1,0:T(8,128)} %get-tuple-element.39) | data formatting | bytes 15925248 | tf_op jit(solution)/shard_map/convert_element_type | solution.py:241
  1034.8 12.8 %copy.132 = f32[8,288,4,216]{3,0,2,1:T(8,128)} copy(f32[8,288,4,216]{3,2,1,0:T(4,128)} %reshape.477) | data formatting | bytes 15925248 | tf_op jit(solution)/shard_map/convert_element_type | solution.py:241
  1047.5 10.8 reshape.475
  1058.3 12.9 %reshape.476 = f32[8,288,4,216]{3,2,1,0:T(4,128)} reshape(f32[8,288,864]{2,1,0:T(8,128)} %get-tuple-element.40) | data formatting | bytes 15925248 | tf_op jit(solution)/shard_map/convert_element_type | solution.py:241
  1071.2 12.8 %copy.133 = f32[8,288,4,216]{3,0,2,1:T(8,128)} copy(f32[8,288,4,216]{3,2,1,0:T(4,128)} %reshape.476) | data formatting | bytes 15925248 | tf_op jit(solution)/shard_map/convert_element_type | solution.py:241
  1084.0 10.8 reshape.474
  (238 shorter events, 45.6 us)
Async XLA Ops:
  7.2 84.8 %copy-start = (bf16[256,1152]{1,0:T(8,128)(2,1)S(1)}, bf16[256,1152]{1,0:T(8,128)(2,1)}, u32[]{:S(2)}) copy-start(bf16[256,1152]{1,0:T(8,128)(2,1)} %param.24) | copy-start | bytes 1769476
  7.2 70.0 %all-gather.30.cloned.1.call-start = ((), (), s32[]{:S(2)}) async-start(), calls=%async_computation.21 | async-start | bytes 4055040 | tf_op jit(solution)/shard_map/all_gather | solution.py:115
  13.2 105.5 %all-gather.14.cloned.1.call-start = ((), (), s32[]{:S(2)}) async-start(), calls=%async_computation.7 | async-start | bytes 2359296 | tf_op jit(solution)/shard_map/all_gather | solution.py:188
  17.1 72.8 %copy-start.47 = (f32[256]{0:T(256)}, f32[256]{0:T(256)S(1)}, u32[]{:S(2)}) copy-start(f32[256]{0:T(256)S(1)} %get-tuple-element.34) | copy-start | bytes 3076
  19.0 66.3 %copy-start.56 = (f32[256]{0:T(256)}, f32[256]{0:T(256)S(1)}, u32[]{:S(2)}) copy-start(f32[256]{0:T(256)S(1)} %fusion.84) | copy-start | bytes 3076
  79.5 5.8 copy-start.30
  79.5 5.8 copy-start.10
  88.5 9.8 copy-start.12
  91.1 13.5 %copy-start.16 = (f32[256,128]{1,0:T(8,128)}, f32[256,128]{1,0:T(8,128)S(1)}, u32[]{:S(2)}) copy-start(f32[256,128]{1,0:T(8,128)S(1)} %get-tuple-element.68) | copy-start | bytes 393220
  91.2 13.5 %copy-start.18 = (f32[256,128]{1,0:T(8,128)}, f32[256,128]{1,0:T(8,128)S(1)}, u32[]{:S(2)}) copy-start(f32[256,128]{1,0:T(8,128)S(1)} %get-tuple-element.69) | copy-start | bytes 393220
  92.0 87.5 %all-gather.16.cloned.1.call-start = ((), (), s32[]{:S(2)}) async-start(), calls=%async_computation.8 | async-start | bytes 2433024 | tf_op jit(solution)/shard_map/all_gather | solution.py:127
  92.7 167.3 %all-gather.20.cloned.1.call-start = ((), (), s32[]{:S(2)}) async-start(), calls=%async_computation.10 | async-start | bytes 5160960 | tf_op jit(solution)/shard_map/all_gather | solution.py:149
  92.8 8.2 copy-start.55
  92.8 9.1 copy-start.32
  98.4 201.4 %all-gather.18.cloned.1.call-start = ((), (), s32[]{:S(2)}) async-start(), calls=%async_computation.9 | async-start | bytes 5308416 | tf_op jit(solution)/shard_map/all_gather | solution.py:208
  100.9 3.9 copy-start.4
  101.0 3.8 copy-start.37
  104.4 17.5 %copy-start.28 = (f32[256,4]{0,1:T(4,128)}, f32[256,4]{0,1:T(4,128)S(1)}, u32[]{:S(2)}) copy-start(f32[256,4]{0,1:T(4,128)S(1)} %copy.91) | copy-start | bytes 12292
  104.4 17.5 %copy-start.26 = (f32[256,4]{0,1:T(4,128)}, f32[256,4]{0,1:T(4,128)S(1)}, u32[]{:S(2)}) copy-start(f32[256,4]{0,1:T(4,128)S(1)} %fusion.83) | copy-start | bytes 12292
  104.9 17.1 %copy-start.22 = (bf16[256,4,256]{2,0,1:T(8,128)(2,1)}, bf16[256,4,256]{2,0,1:T(8,128)(2,1)S(1)}, u32[]{:S(2)}) copy-start(bf16[256,4,256]{2,0,1:T(8,128)(2,1)S(1)} %fusion.44) | copy-start | bytes 1572868
  122.0 3.5 copy-start.20
  126.8 56.8 %copy-start.14 = (bf16[4,256,256]{1,2,0:T(8,128)(2,1)}, bf16[4,256,256]{1,2,0:T(8,128)(2,1)S(1)}, u32[]{:S(2)}) copy-start(bf16[4,256,256]{1,2,0:T(8,128)(2,1)S(1)} %convolution_convert_fusion.7) | copy-start | bytes 1572868
  182.1 131.0 %copy-start.33 = (f32[256]{0:T(256)}, f32[256]{0:T(256)S(1)}, u32[]{:S(2)}) copy-start(f32[256]{0:T(256)S(1)} %fusion.86) | copy-start | bytes 3076
  182.6 130.5 %copy-start.46 = (f32[256]{0:T(256)}, f32[256]{0:T(256)S(1)}, u32[]{:S(2)}) copy-start(f32[256]{0:T(256)S(1)} %get-tuple-element.32) | copy-start | bytes 3076
  182.6 130.5 %copy-start.41 = (f32[256]{0:T(256)}, f32[256]{0:T(256)S(1)}, u32[]{:S(2)}) copy-start(f32[256]{0:T(256)S(1)} %fusion.87) | copy-start | bytes 3076
  183.7 162.2 %all-gather.22.cloned.1.call-start = ((), (), s32[]{:S(2)}) async-start(), calls=%async_computation.11 | async-start | bytes 2488320 | tf_op jit(solution)/shard_map/all_gather | solution.py:155
  185.6 222.4 %reduce-scatter.10.cloned.1.call-start = ((), (), s32[]{:S(2)}) async-start(), calls=%async_computation.12 | async-start | bytes 5308416 | tf_op jit(solution)/shard_map/reduce_scatter | solution.py:216
  313.1 5.2 copy-start.6
  355.1 54.1 %copy-start.11 = (bf16[1,256,1152]{2,1,0:T(8,128)(2,1)S(1)}, bf16[1,256,1152]{2,1,0:T(8,128)(2,1)}, u32[]{:S(2)}) copy-start(bf16[1,256,1152]{2,1,0:T(8,128)(2,1)} %param.20) | copy-start | bytes 1769476
  355.1 97.6 %all-gather.24.cloned.1.call-start = ((), (), s32[]{:S(2)}) async-start(), calls=%async_computation.13 | async-start | bytes 5308416 | tf_op jit(solution)/shard_map/all_gather | solution.py:223
  413.7 122.7 %reduce-scatter.12.cloned.1.call-start = ((), (), s32[]{:S(2)}) async-start(), calls=%async_computation.14 | async-start | bytes 5308416 | tf_op jit(solution)/shard_map/reduce_scatter | solution.py:228
  452.8 18.1 %copy-start.59 = (bf16[1152,1792]{1,0:T(8,128)(2,1)S(1)}, bf16[1152,1792]{1,0:T(8,128)(2,1)}, u32[]{:S(2)}) copy-start(bf16[1152,1792]{1,0:T(8,128)(2,1)} %all-gather.20.cloned.1.call-done) | copy-start | bytes 12386308
  482.3 98.1 %reduce-scatter.22.cloned.1.call-start = ((), (), s32[]{:S(2)}) async-start(), calls=%async_computation.22 | async-start | bytes 2488320
  490.9 48.2 %copy-start.9 = (bf16[256,1152]{1,0:T(8,128)(2,1)S(1)}, bf16[256,1152]{1,0:T(8,128)(2,1)}, u32[]{:S(2)}) copy-start(bf16[256,1152]{1,0:T(8,128)(2,1)} %reduce-scatter.10.cloned.1.call-done) | copy-start | bytes 1769476
  492.4 132.7 %reduce-scatter.14.cloned.1.call-start = ((), (), s32[]{:S(2)}) async-start(), calls=%async_computation.15 | async-start | bytes 2359296 | tf_op jit(solution)/shard_map/reduce_scatter | solution.py:266
  536.3 6.4 copy-start.54
  536.3 6.5 copy-start.34
  539.1 4.0 copy-start.13
  542.8 3.1 copy-start.3
  542.8 3.8 copy-start.21
  551.0 3.6 copy-start.25
  557.5 146.3 %reduce-scatter.20.cloned.1.call-start = ((), (), s32[]{:S(2)}) async-start(), calls=%async_computation.18 | async-start | bytes 5160960 | tf_op jit(solution)/shard_map/reduce_scatter | solution.py:234
  572.9 7.9 copy-start.43
  572.9 8.0 copy-start.44
  572.9 8.1 copy-start.45
  572.9 235.6 %reduce-scatter.18.cloned.1.call-start = ((), (), s32[]{:S(2)}) async-start(), calls=%async_computation.17 | async-start | bytes 2433024 | tf_op jit(solution)/shard_map/reduce_scatter | solution.py:249
  576.2 269.1 %all-gather.26.cloned.1.call-start = ((), (), s32[]{:S(2)}) async-start(), calls=%async_computation.19 | async-start | bytes 4478976 | tf_op jit(solution)/shard_map/all_gather | solution.py:235
  580.4 375.7 %reduce-scatter.16.cloned.1.call-start = ((), (), s32[]{:S(2)}) async-start(), calls=%async_computation.16 | async-start | bytes 4055040 | tf_op jit(solution)/shard_map/reduce_scatter | solution.py:311
  581.1 3.9 copy-start.17
  581.1 3.9 copy-start.19
  581.1 4.1 copy-start.5
  581.1 4.1 copy-start.27
  581.1 4.1 copy-start.38
  585.2 42.0 %copy-start.48 = (f32[256]{0:T(256)S(1)}, f32[256]{0:T(256)}, u32[]{:S(2)}) copy-start(f32[256]{0:T(256)} %copy-done.47) | copy-start | bytes 3076
  585.2 42.0 %copy-start.58 = (f32[128]{0:T(128)S(1)}, f32[128]{0:T(128)}, u32[]{:S(2)}) copy-start(f32[128]{0:T(128)} %negate_power_fusion) | copy-start | bytes 1540
  585.2 42.6 %copy-start.36 = (f32[256]{0:T(256)S(1)}, f32[256]{0:T(256)}, u32[]{:S(2)}) copy-start(f32[256]{0:T(256)} %copy-done.35) | copy-start | bytes 3076
  585.2 42.6 %copy-start.40 = (f32[256]{0:T(256)S(1)}, f32[256]{0:T(256)}, u32[]{:S(2)}) copy-start(f32[256]{0:T(256)} %copy-done.39) | copy-start | bytes 3076
  585.2 43.7 %copy-start.52 = (f32[256]{0:T(256)S(1)}, f32[256]{0:T(256)}, u32[]{:S(2)}) copy-start(f32[256]{0:T(256)} %copy-done.51) | copy-start | bytes 3076
  585.7 44.4 %copy-start.31 = (f32[1152]{0:T(1024)S(1)}, f32[1152]{0:T(1024)}, u32[]{:S(2)}) copy-start(f32[1152]{0:T(1024)} %copy-done.30) | copy-start | bytes 13828
  585.7 44.4 %copy-start.57 = (f32[256]{0:T(256)S(1)}, f32[256]{0:T(256)}, u32[]{:S(2)}) copy-start(f32[256]{0:T(256)} %copy-done.56) | copy-start | bytes 3076
  647.8 171.9 %copy-start.50 = (f32[256]{0:T(256)S(1)}, f32[256]{0:T(256)}, u32[]{:S(2)}) copy-start(f32[256]{0:T(256)} %copy-done.49) | copy-start | bytes 3076
  647.8 172.6 %copy-start.8 = (f32[256,1152]{1,0:T(8,128)S(1)}, f32[256,1152]{1,0:T(8,128)}, u32[]{:S(2)}) copy-start(f32[256,1152]{1,0:T(8,128)} %copy-done.7) | copy-start | bytes 3538948
  647.9 363.2 %all-gather.28.cloned.1.call-start = ((), (), s32[]{:S(2)}) async-start(), calls=%async_computation.20 | async-start | bytes 9289728 | tf_op jit(solution)/shard_map/all_gather | solution.py:236
  1084.0 10.8 copy-start.1
  (14 other events, 18.7 us)
Sparse Core Ops, SparseCore 0:
  13.3 63.8 all-gather.29
  92.1 26.5 all-gather.13
  122.2 57.2 all-gather.15
  181.4 78.5 all-gather.19
  262.3 37.4 all-gather.17
  301.8 43.9 all-gather.21
  355.2 52.6 reduce-scatter.9
  413.8 38.8 all-gather.23
  482.4 53.8 reduce-scatter.11
  538.5 41.8 reduce-scatter.21
  584.2 40.8 reduce-scatter.13
  628.0 75.7 reduce-scatter.19
  709.1 99.4 reduce-scatter.17
  810.4 34.8 all-gather.25
  852.0 103.9 reduce-scatter.15
  957.9 53.1 all-gather.27

commit v2 on v1

--- a/solution.py
+++ b/solution.py
@@ -1,6 +1,8 @@
 import jax
 import jax.numpy as jnp
 from jax import lax
+from jax.experimental import pallas as pl
+from jax.experimental.pallas import tpu as pltpu
 from jax.sharding import PartitionSpec as P
 
 EPS = 1e-06
@@ -71,6 +73,85 @@
     return lax.dot_general(
         left_side, right_side, (((0,), (0,)), ((), ())), preferred_element_type=jnp.float32
     )
+
+
+def shifted(values, step, count):
+    return lax.ppermute(values, "fsdp", [(i, (i + step) % count) for i in range(count)])
+
+
+def send_piece(piece):
+    count = lax.axis_size("fsdp")
+    return [shifted(piece, step, count) for step in range(1, count)]
+
+
+def stack_pieces(piece, received):
+    count = lax.axis_size("fsdp")
+    me = lax.axis_index("fsdp")
+    whole = jnp.zeros((count, *piece.shape), piece.dtype)
+    whole = lax.dynamic_update_index_in_dim(whole, piece, me, 0)
+    for step, got in enumerate(received, 1):
+        whole = lax.dynamic_update_index_in_dim(whole, got, lax.rem(me - step + count, count), 0)
+    return whole
+
+
+def gather_fsdp(piece):
+    return stack_pieces(piece, send_piece(piece))
+
+
+def after(value, received, index):
+    value, received[index] = lax.optimization_barrier((value, received[index]))
+    return value
+
+
+def send_chunks(chunks):
+    count = lax.axis_size("fsdp")
+    me = lax.axis_index("fsdp")
+    received = []
+    for step in range(1, count):
+        sent = lax.dynamic_index_in_dim(chunks, lax.rem(me + step, count), 0, keepdims=False)
+        received.append(shifted(sent, step, count))
+    return received
+
+
+def own_total(chunks, received):
+    me = lax.axis_index("fsdp")
+    total = lax.dynamic_index_in_dim(chunks, me, 0, keepdims=False).astype(jnp.float32)
+    for got in received:
+        total = total + got.astype(jnp.float32)
+    return total
+
+
+def sum_fsdp(chunks):
+    return own_total(chunks, send_chunks(chunks))
+
+
+def unit_order(pieces, fsdp_count, unit_piece, unit_pad):
+    ctx_count, rows, cols = pieces.shape
+    units = ctx_count * fsdp_count * unit_piece
+    block = 32 if rows % 32 == 0 else rows
+
+    def kernel(in_ref, gate_ref, up_ref):
+        for out_ref, base in ((gate_ref, 0), (up_ref, unit_pad)):
+            held = [
+                in_ref[c, :, base : base + unit_pad].astype(jnp.float32) for c in range(ctx_count)
+            ]
+            for pair in range(fsdp_count // 2):
+                parts = [
+                    held[c][:, f * unit_piece : (f + 1) * unit_piece]
+                    for f in (2 * pair, 2 * pair + 1)
+                    for c in range(ctx_count)
+                ]
+                span = units * 2 // fsdp_count
+                out_ref[:, pair * span : (pair + 1) * span] = jnp.concatenate(parts, axis=1)
+
+    return pl.pallas_call(
+        kernel,
+        grid=(rows // block,),
+        in_specs=[pl.BlockSpec((ctx_count, block, cols), lambda i: (0, i, 0))],
+        out_specs=[pl.BlockSpec((block, units), lambda i: (i, 0))] * 2,
+        out_shape=[jax.ShapeDtypeStruct((rows, units), jnp.float32)] * 2,
+        compiler_params=pltpu.CompilerParams(vmem_limit_bytes=40 * 1024 * 1024),
+    )(pieces)
 
 
 def per_device(
@@ -112,11 +193,10 @@
     qkv_send = jnp.concatenate(
         [lax.dynamic_slice_in_dim(qkv_own, ctx_index * qkv_piece, qkv_piece), gain_row], axis=0
     )
-    qkv_got = lax.all_gather(qkv_send, ("fsdp", "ctx"), axis=0).reshape(
-        fsdp_count, ctx_count, qkv_piece + 1, qkv_cols
-    )
-    qkv_full = qkv_got[:, :, :qkv_piece].reshape(-1, qkv_cols)
-    gains_got = qkv_got[:, 0, qkv_piece].astype(jnp.float32)
+    qkv_layers = gather_fsdp(qkv_send)
+    gains_got = qkv_layers[:, qkv_piece].astype(jnp.float32)
+    qkv_got = lax.all_gather(qkv_layers[:, :qkv_piece], "ctx", axis=0)
+    qkv_full = jnp.transpose(qkv_got, (1, 0, 2, 3)).reshape(-1, qkv_cols)
     gain_full = []
     at = 0
     for size in gain_sizes:
@@ -124,12 +204,11 @@
         at += size
     input_gain, query_gain, key_gain, attn_gain, pre_gain, post_gain = gain_full
     out_piece = out_proj.shape[0] // ctx_count
-    out_full = lax.all_gather(
-        lax.dynamic_slice_in_dim(out_proj, ctx_index * out_piece, out_piece),
-        ("fsdp", "ctx"),
-        axis=0,
-        tiled=True,
-    )
+    out_layers = gather_fsdp(
+        lax.dynamic_slice_in_dim(out_proj, ctx_index * out_piece, out_piece)
+    )
+    out_got = lax.all_gather(out_layers, "ctx", axis=0)
+    out_full = jnp.transpose(out_got, (1, 0, 2, 3)).reshape(-1, width)
 
     unit_rows = down_proj.shape[0]
     unit_piece = unit_rows // ctx_count
@@ -146,18 +225,11 @@
         parts.append(jnp.zeros((weight.shape[0], unit_pad - unit_own), weight.dtype))
         return jnp.concatenate(parts, axis=1)
 
-    gate_up = lax.all_gather(
-        jnp.concatenate([unit_columns(gate_proj), unit_columns(up_proj)], axis=1),
-        "fsdp",
-        axis=0,
-        tiled=True,
-    )
-    down_own = lax.all_gather(
-        lax.dynamic_slice_in_dim(down_proj, ctx_index * unit_piece, unit_piece),
-        "fsdp",
-        axis=0,
-        tiled=True,
-    )
+    gate_up_own = jnp.concatenate([unit_columns(gate_proj), unit_columns(up_proj)], axis=1)
+    gate_up_got = send_piece(gate_up_own)
+    down_own = gather_fsdp(
+        lax.dynamic_slice_in_dim(down_proj, ctx_index * unit_piece, unit_piece)
+    ).reshape(unit_own, width)
     down_own = jnp.pad(down_own, ((0, unit_pad - unit_own), (0, 0)))
 
     places, second, in_seq = positions_of(dealing[0], lengths[0], tok_rows)
@@ -193,6 +265,7 @@
     )
     key_all, value_all = kv_all[:, :head_width], kv_all[:, head_width:]
     heads = head_cols // head_width
+    query_rows = after(query_rows, gate_up_got, 0)
     scores = dot_last(query_rows, key_all).reshape(heads, tok_rows, -1)
     weights = jnp.where(allowed[None], jnp.exp(scores), 0.0)
     totals = jnp.sum(weights, axis=-1, keepdims=True)
@@ -201,11 +274,13 @@
         heads, tok_rows, head_width
     )
     attn_bf = jnp.transpose(attn_heads, (1, 0, 2)).reshape(tok_rows, -1).astype(jnp.bfloat16)
+    attn_bf = after(attn_bf, gate_up_got, 1)
     attn_proj = jnp.dot(attn_bf, out_full, preferred_element_type=jnp.float32)
     attn_normed, attn_pull = jax.vjp(scaled, attn_proj, attn_gain)
     hidden = inputs + attn_normed
     normed_mid, mid_pull = jax.vjp(scaled, hidden, pre_gain)
     mid_all = lax.all_gather(normed_mid.astype(jnp.bfloat16), "ctx", axis=0, tiled=True)
+    gate_up = stack_pieces(gate_up_own, gate_up_got).reshape(width, 2 * unit_pad)
     gate_up_act = jnp.dot(mid_all, gate_up, preferred_element_type=jnp.float32)
     gate_act, up_act = gate_up_act[:, :unit_pad], gate_up_act[:, unit_pad:]
     glu_value, glu_pull = jax.vjp(
@@ -230,28 +305,21 @@
     ).astype(jnp.float32)
     grad_down = dot_first(glu_bf, d_mlp_all)[:unit_own].astype(jnp.bfloat16)
     grad_gate_up = dot_first(mid_all, d_gate_up).astype(jnp.bfloat16)
-    grad_down = lax.psum_scatter(grad_down, "fsdp", scatter_dimension=0, tiled=True)
-    grad_gate_up = lax.psum_scatter(grad_gate_up, "fsdp", scatter_dimension=0, tiled=True)
-    grad_down = lax.all_gather(grad_down, "ctx", axis=0, tiled=True).astype(jnp.float32)
-    grad_gate_up = lax.all_gather(grad_gate_up, "ctx", axis=0)
-
-    def unit_order(pieces):
-        rows = pieces.shape[1]
-        pieces = pieces.reshape(ctx_count, rows, fsdp_count, unit_piece)
-        return jnp.transpose(pieces, (1, 2, 0, 3)).reshape(rows, -1).astype(jnp.float32)
-
-    grad_gate = unit_order(grad_gate_up[:, :, :unit_own])
-    grad_up = unit_order(grad_gate_up[:, :, unit_pad : unit_pad + unit_own])
+    grad_down_chunks = grad_down.reshape(fsdp_count, unit_piece, width)
+    grad_gate_up_chunks = grad_gate_up.reshape(fsdp_count, -1, 2 * unit_pad)
+    grad_down_got = send_chunks(grad_down_chunks)
+    grad_gate_up_got = send_chunks(grad_gate_up_chunks)
+    d_mid, _, _ = lax.optimization_barrier((d_mid, grad_down, grad_gate_up))
     d_hidden_part, d_pre_gain = mid_pull(d_mid)
     d_hidden = d_out + d_hidden_part
     d_attn_proj, d_attn_gain = attn_pull(d_hidden)
     d_proj_bf = d_attn_proj.astype(jnp.bfloat16)
-    grad_out = lax.psum_scatter(
-        dot_first(attn_bf, d_proj_bf).astype(jnp.bfloat16),
-        ("fsdp", "ctx"),
-        scatter_dimension=0,
-        tiled=True,
-    )
+    out_terms = dot_first(attn_bf, d_proj_bf).astype(jnp.bfloat16)
+    out_terms = jnp.transpose(
+        out_terms.reshape(fsdp_count, ctx_count, out_piece, width), (1, 0, 2, 3)
+    ).reshape(-1, width)
+    out_sum = lax.psum_scatter(out_terms, "ctx", scatter_dimension=0, tiled=True)
+    grad_out = sum_fsdp(out_sum.reshape(fsdp_count, out_piece, width)).astype(jnp.bfloat16)
     grad_out = lax.all_gather(grad_out, "ctx", axis=0, tiled=True).astype(jnp.float32)
     d_attn_bf = dot_last(d_proj_bf, out_full).astype(jnp.bfloat16)
     d_rows = jnp.transpose(d_attn_bf.reshape(tok_rows, -1, head_width), (1, 0, 2)).reshape(
@@ -263,8 +331,10 @@
     d_scores = (probs * (d_probs - inner_sum)).astype(jnp.bfloat16)
     key_grad = dot_first(d_scores, query_rows)
     value_grad = dot_first(probs_bf, d_rows)
+    kv_terms = jnp.concatenate([key_grad, value_grad], axis=1).astype(jnp.bfloat16)
+    kv_terms = after(kv_terms, grad_gate_up_got, 0)
     kv_own = lax.psum_scatter(
-        jnp.concatenate([key_grad, value_grad], axis=1).astype(jnp.bfloat16),
+        kv_terms,
         "ctx",
         scatter_dimension=0,
         tiled=True,
@@ -276,6 +346,7 @@
         (1, 0, 2),
     )
     d_query_raw, d_query_gain = query_pull(d_query)
+    kv_own = after(kv_own, grad_gate_up_got, 1)
     d_key_raw, d_key_gain = key_pull(kv_own[:, :head_width])
     d_qkv_bf = jnp.concatenate([d_query_raw, d_key_raw, kv_own[:, head_width:]], axis=1).astype(
         jnp.bfloat16
@@ -299,18 +370,33 @@
         axis=1,
     ).astype(jnp.bfloat16)
     gain_grads = jnp.pad(gain_grads, ((0, 0), (0, qkv_cols - gain_grads.shape[1])))
+    qkv_slot = -(-(qkv_piece + 1) // 8) * 8
     qkv_terms = jnp.concatenate(
         [
             grad_qkv.reshape(fsdp_count, ctx_count, qkv_piece, qkv_cols),
             jnp.broadcast_to(
                 gain_grads[:, None, None], (fsdp_count, ctx_count, 1, qkv_cols)
             ),
+            jnp.zeros(
+                (fsdp_count, ctx_count, qkv_slot - qkv_piece - 1, qkv_cols), jnp.bfloat16
+            ),
         ],
         axis=2,
-    ).reshape(fsdp_count * ctx_count, qkv_piece + 1, qkv_cols)
-    qkv_sum = lax.psum_scatter(qkv_terms, ("fsdp", "ctx"), scatter_dimension=0, tiled=True)[0]
-    gain_sum = qkv_sum[qkv_piece].astype(jnp.float32)
-    grad_qkv = lax.all_gather(qkv_sum[:qkv_piece], "ctx", axis=0, tiled=True).astype(jnp.float32)
+    )
+    qkv_terms = jnp.transpose(qkv_terms, (1, 0, 2, 3)).reshape(-1, qkv_cols)
+    qkv_terms = after(qkv_terms, grad_gate_up_got, 2)
+    qkv_sum = lax.psum_scatter(qkv_terms, "ctx", scatter_dimension=0, tiled=True)
+    qkv_sum = sum_fsdp(qkv_sum.reshape(fsdp_count, qkv_slot, qkv_cols)[:, : qkv_piece + 1])
+    gain_sum = qkv_sum[qkv_piece]
+    grad_qkv = lax.all_gather(
+        qkv_sum[:qkv_piece].astype(jnp.bfloat16), "ctx", axis=0, tiled=True
+    ).astype(jnp.float32)
+    grad_down = own_total(grad_down_chunks, grad_down_got).astype(jnp.bfloat16)
+    grad_gate_up = own_total(grad_gate_up_chunks, grad_gate_up_got).astype(jnp.bfloat16)
+    grad_down = lax.all_gather(grad_down, "ctx", axis=0, tiled=True).astype(jnp.float32)
+    grad_gate, grad_up = unit_order(
+        lax.all_gather(grad_gate_up, "ctx", axis=0), fsdp_count, unit_piece, unit_pad
+    )
     gain_out = []
     at = 0
     for size in gain_sizes:

time: 1110 us -> 766 us (0.69)
  waiting for transfers between devices: 760 us -> 410 us
  starting transfers between devices: 2.07 us -> 49 us
  local copies, waits for them, and re-layouts: 127 us -> 86.7 us
    reduce_scatter x4 -> x3, waiting for transfers between devices: 304 us -> 27.8 us  [the longest x1 27.8 us: per_device(): lax.psum_scatter(qkv_terms, 'ctx', scatter_dimension=0, tiled=True)]
    ppermute x0 -> x24, waiting for transfers between devices: none -> 203 us  [shifted(): lax.ppermute(values, 'fsdp', [(i, (i + step) % count) for i in range(coun...]
    all_gather x5 -> x3, waiting for transfers between devices: 241 us -> 56.4 us  [the longest x1 33.3 us: per_device(): qkv_got = lax.all_gather(qkv_layers[:, :qkv_piece], 'ctx', axis=0)]
    convert_element_type x6 -> x1, local copies, waits for them, and re-layouts: 72.8 us -> 0.16 us  [per_device(): grad_qkv = lax.all_gather(qkv_sum[:qkv_piece].astype(jnp.bfloat16), 'ctx'...]
    ppermute x0 -> x24, starting transfers between devices: none -> 47.6 us  [shifted(): lax.ppermute(values, 'fsdp', [(i, (i + step) % count) for i in range(coun...]
    all_gather x1, waiting for transfers between devices: 39.8 us -> 0.01 us  [per_device(): lax.all_gather(normed_mid.astype(jnp.bfloat16), 'ctx', axis=0, tiled=True)]
    all_gather x1, waiting for transfers between devices: 23.5 us -> 0.02 us  [per_device(): lax.all_gather(grad_down, 'ctx', axis=0, tiled=True).astype(jnp.float32)]
    reduce_scatter x1, waiting for transfers between devices: 43.9 us -> 24 us  [per_device(): lax.psum_scatter(d_mid_part.astype(jnp.bfloat16), 'ctx', scatter_dimensio...]
  transfers between devices with their start and end apart: 16 -> 36, of which waited for: 16 -> 20; matrix products, arithmetic and copies ran while one was open for 12% -> 19% of each run, Pallas kernels for 0% -> 0%
where the time goes in v2:
time: 766 us; the launch traced here: 758 us
  waiting for transfers between devices  410 us (54%)
  matrix products  107 us (14%)
  local copies, waits for them, and re-layouts  86.7 us (11%)
  other arithmetic  57.1 us (7%)
  starting transfers between devices  49 us (6%)
  blocking collectives  23.5 us (3%)
  between operations  15.8 us (2%)
  Pallas kernels  7.81 us (1%)
    ppermute x24, waiting for transfers between devices, shifted(): lax.ppermute(values, 'fsdp', [(i, (i + step) % count) for i in range(coun...  203 us
    reduce_scatter x1, waiting for transfers between devices, per_device(): lax.psum_scatter(mlp_part.astype(jnp.bfloat16), 'ctx', scatter_dimension=...  60.4 us
    ppermute x24, starting transfers between devices, shifted(): lax.ppermute(values, 'fsdp', [(i, (i + step) % count) for i in range(coun...  47.6 us
    all_gather x1, waiting for transfers between devices, per_device(): lax.all_gather(d_mlp.astype(jnp.bfloat16), 'ctx', axis=0, tiled=True)  38.6 us
    dot_general x6, matrix products, dot_last(): lax.dot_general(left_side, right_side, (((1,), (1,)), ((), ())), preferre...  38.5 us
    dot_general x6, matrix products, dot_first(): lax.dot_general(left_side, right_side, (((0,), (0,)), ((), ())), preferre...  34.5 us
    all_gather x1, waiting for transfers between devices, per_device(): qkv_got = lax.all_gather(qkv_layers[:, :qkv_piece], 'ctx', axis=0)  33.3 us
    reduce_scatter x1, waiting for transfers between devices, per_device(): lax.psum_scatter(qkv_terms, 'ctx', scatter_dimension=0, tiled=True)  27.8 us
  transfers between devices with their start and end apart: 36, of which 20 were waited for; matrix products, arithmetic and copies ran while one was open for 19% of the time, Pallas kernels for 0%

profile of v2, /device:TPU:0, one launch (start us, length us, event | category | flops | bytes accessed | tf_op | source)
XLA Modules:
  0.0 757.5 jit_solution(12106908047726562644)
XLA Ops:
  7.2 4.2 concatenate.39
  12.5 3.1 collective-permute-start
  15.6 2.6 collective-permute-start.1
  19.5 2.3 collective-permute-done
  21.9 4.4 collective-permute-done.1
  31.5 33.3 %all-gather.21.cloned.1.call-done = bf16[32,36,1536]{2,1,0:T(8,128)(2,1)} async-done(((bf16[4,36,1536]{2,1,0:T(8,128)(2,1)}), bf16[32,36,1536]{2,1,0:T(8,128)(2,1)}) %all-gather.21.cloned.1.call-update) | async-done | bytes 3538960 | tf_op jit(solution)/shard_map/all_gather | solution.py:198
  64.8 3.9 copy.150
  68.7 3.9 copy.110
  72.6 5.7 reshape.489
  78.3 3.2 fusion.60
  87.1 2.4 collective-permute-start.6
  92.4 2.7 collective-permute-done.6
  101.1 2.7 collective-permute-start.3
  109.7 40.1 %collective-permute-done.3 = bf16[288,1792]{1,0:T(8,128)(2,1)} collective-permute-done((bf16[288,1792]{1,0:T(8,128)(2,1)}, bf16[288,1792]{1,0:T(8,128)(2,1)}, u32[]{:S(2)}, u32[]{:S(2)}) %collective-permute-start.3) | collective-permute-done | bytes 1032224 | tf_op jit(solution)/shard_map/ppermute | solution.py:79
  149.8 3.3 fusion.2
  158.7 11.5 %collective-permute-done.4 = bf16[288,1792]{1,0:T(8,128)(2,1)} collective-permute-done((bf16[288,1792]{1,0:T(8,128)(2,1)}, bf16[288,1792]{1,0:T(8,128)(2,1)}, u32[]{:S(2)}, u32[]{:S(2)}) %collective-permute-start.4) | collective-permute-done | bytes 1032224 | tf_op jit(solution)/shard_map/ppermute | solution.py:79
  170.2 2.6 multiply_reduce_fusion.5
  177.9 10.2 %collective-permute-start.10 = (bf16[216,1152]{1,0:T(8,128)(2,1)S(1)}, bf16[216,1152]{1,0:T(8,128)(2,1)S(1)}, u32[]{:S(2)}, u32[]{:S(2)}) collective-permute-start(bf16[216,1152]{1,0:T(8,128)(2,1)S(1)} %get-tuple-element.59), channel_id=1, source_target_pairs={{0,2},{1,3},{2,0},{3,1},{4,6},{5,7},{6,4},{7,5},{8,10},{9,11},{10,... | collective-permute-start | bytes 1493000 | tf_op jit(solution)/shard_map/ppermute | solution.py:79
  192.1 2.3 broadcast_in_dim.170
  194.3 2.2 bitcast_dynamic-update-slice_fusion.3
  196.6 34.8 %collective-permute-done.9 = bf16[216,1152]{1,0:T(8,128)(2,1)S(1)} collective-permute-done((bf16[216,1152]{1,0:T(8,128)(2,1)S(1)}, bf16[216,1152]{1,0:T(8,128)(2,1)S(1)}, u32[]{:S(2)}, u32[]{:S(2)}) %collective-permute-start.9) | collective-permute-done | bytes 497696 | tf_op jit(solution)/shard_map/ppermute | solution.py:79
  232.2 8.3 %collective-permute-done.10 = bf16[216,1152]{1,0:T(8,128)(2,1)S(1)} collective-permute-done((bf16[216,1152]{1,0:T(8,128)(2,1)S(1)}, bf16[216,1152]{1,0:T(8,128)(2,1)S(1)}, u32[]{:S(2)}, u32[]{:S(2)}) %collective-permute-start.10) | collective-permute-done | bytes 497696 | tf_op jit(solution)/shard_map/ppermute | solution.py:79
  242.2 2.2 bitcast_dynamic-update-slice_fusion.2
  244.4 2.2 bitcast_dynamic-update-slice_fusion.1
  247.7 13.3 %fusion.110 = f32[2048,1792]{0,1:T(8,128)S(1)} fusion(bf16[2048,1152]{1,0:T(8,128)(2,1)} %all-gather.15.cloned.1.call-done, bf16[1152,1792]{1,0:T(8,128)(2,1)} %bitcast.29), kind=kOutput, calls=%fused_computation.253 | convolution fusion | flops 8455716864 | bytes 23527424 | tf_op jit(solution)/shard_map/dot_general | solution.py:284
  261.0 2.6 multiply_convert_fusion.3
  263.5 2.6 copy-done.6
  268.0 8.8 %convolution_convert_fusion = bf16[2048,1152]{1,0:T(8,128)(2,1)} fusion(bf16[2048,896]{0,1:T(8,128)(2,1)S(1)} %multiply_convert_fusion.3, bf16[864,1152]{1,0:T(8,128)(2,1)} %bitcast.34), kind=kOutput, calls=%fused_computation.10 | convolution fusion | flops 4230217728 | bytes 10379264 | tf_op jit(solution)/shard_map/dot_general | solution.py:290
  276.9 60.4 %reduce-scatter.6.cloned.1.call-done = bf16[256,1152]{1,0:T(8,128)(2,1)} async-done(((bf16[2048,1152]{1,0:T(8,128)(2,1)}), bf16[256,1152]{1,0:T(8,128)(2,1)}) %reduce-scatter.6.cloned.1.call-update) | async-done | bytes 589840 | tf_op jit(solution)/shard_map/reduce_scatter | solution.py:291
  338.6 2.2 fusion.43
  340.8 2.2 fusion.39
  343.5 38.6 %all-gather.17.cloned.1.call-done = bf16[2048,1152]{1,0:T(8,128)(2,1)} async-done(((bf16[256,1152]{1,0:T(8,128)(2,1)}), bf16[2048,1152]{1,0:T(8,128)(2,1)}) %all-gather.17.cloned.1.call-update) | async-done | bytes 4718608 | tf_op jit(solution)/shard_map/all_gather | solution.py:298
  382.1 15.1 %fusion.9 = (bf16[2048,896]{0,1:T(8,128)(2,1)S(1)}, bf16[2048,896]{0,1:T(8,128)(2,1)S(1)}) fusion(f32[2048,1792]{0,1:T(8,128)} %copy-done.6, bf16[2048,1152]{1,0:T(8,128)(2,1)} %all-gather.17.cloned.1.call-done, bf16[864,1152]{1,0:T(8,128)(2,1)} %bitcast.34), kind=kOutput, calls=%fused_computation.20 | convolution fusion | flops 4271898624 | bytes 28729344 | tf_op jit(solution)/shard_map/dot_general | solution.py:67
  400.1 13.6 %convolution_convert_fusion.2 = bf16[2048,1152]{1,0:T(8,128)(2,1)} fusion(bf16[1152,1792]{1,0:T(8,128)(2,1)} %bitcast.29, bf16[2048,896]{0,1:T(8,128)(2,1)S(1)} %get-tuple-element.70, bf16[2048,896]{0,1:T(8,128)(2,1)S(1)} %get-tuple-element.69), kind=kOutput, calls=%fused_computation.12 | convolution fusion | flops 8472756224 | bytes 16187392 | tf_op jit(solution)/shard_map/dot_general | solution.py:67
  414.5 8.5 %fusion.111 = bf16[896,1152]{1,0:T(8,128)(2,1)S(1)} fusion(bf16[2048,896]{0,1:T(8,128)(2,1)} %copy-done.14, bf16[2048,1152]{1,0:T(8,128)(2,1)} %all-gather.17.cloned.1.call-done), kind=kOutput, calls=%fused_computation.254 | convolution fusion | flops 4227858432 | bytes 10452992 | tf_op jit(solution)/shard_map/dot_general | solution.py:73
  426.2 12.1 %convolution_convert_fusion.3 = bf16[1152,1792]{1,0:T(8,128)(2,1)S(1)} fusion(bf16[2048,1152]{1,0:T(8,128)(2,1)} %all-gather.15.cloned.1.call-done, bf16[2048,896]{0,1:T(8,128)(2,1)S(1)} %copy-done.67, bf16[2048,896]{0,1:T(8,128)(2,1)S(1)} %copy-done.65), kind=kOutput, calls=%fused_computation.13 | convolution fusion | flops 8472461312 | bytes 16187392 | tf_op jit(solution)/shard_map/dot_general | solution.py:73
  443.7 24.0 %reduce-scatter.8.cloned.1.call-done = bf16[256,1152]{1,0:T(8,128)(2,1)} async-done(((bf16[2048,1152]{1,0:T(8,128)(2,1)}), bf16[256,1152]{1,0:T(8,128)(2,1)}) %reduce-scatter.8.cloned.1.call-update) | async-done | bytes 589840 | tf_op jit(solution)/shard_map/reduce_scatter | solution.py:303
  469.9 3.7 multiply_reduce_fusion.1
  478.3 3.0 fusion.1
  481.3 3.6 convolution_convert_fusion.5
  485.0 5.2 fusion.15
  494.2 2.3 collective-permute-start.23
  497.1 11.7 %collective-permute-done.21 = bf16[216,1152]{1,0:T(8,128)(2,1)S(1)} collective-permute-done((bf16[216,1152]{1,0:T(8,128)(2,1)S(1)}, bf16[216,1152]{1,0:T(8,128)(2,1)S(1)}, u32[]{:S(2)}, u32[]{:S(2)}) %collective-permute-start.21) | collective-permute-done | bytes 497696 | tf_op jit(solution)/shard_map/ppermute | solution.py:79
  508.7 8.9 %collective-permute-done.23 = bf16[216,1152]{1,0:T(8,128)(2,1)S(1)} collective-permute-done((bf16[216,1152]{1,0:T(8,128)(2,1)S(1)}, bf16[216,1152]{1,0:T(8,128)(2,1)S(1)}, u32[]{:S(2)}, u32[]{:S(2)}) %collective-permute-start.23) | collective-permute-done | bytes 497696 | tf_op jit(solution)/shard_map/ppermute | solution.py:79
  517.6 21.9 %collective-permute-done.22 = bf16[216,1152]{1,0:T(8,128)(2,1)S(1)} collective-permute-done((bf16[216,1152]{1,0:T(8,128)(2,1)S(1)}, bf16[216,1152]{1,0:T(8,128)(2,1)S(1)}, u32[]{:S(2)}, u32[]{:S(2)}) %collective-permute-start.22) | collective-permute-done | bytes 497696 | tf_op jit(solution)/shard_map/ppermute | solution.py:79
  546.5 5.0 convolution_multiply_fusion
  557.1 50.9 %collective-permute-done.13 = bf16[288,1792]{1,0:T(8,128)(2,1)} collective-permute-done((bf16[288,1792]{1,0:T(8,128)(2,1)}, bf16[288,1792]{1,0:T(8,128)(2,1)}, u32[]{:S(2)}, u32[]{:S(2)}) %collective-permute-start.13) | collective-permute-done | bytes 1032224 | tf_op jit(solution)/shard_map/ppermute | solution.py:79
  611.1 4.3 fusion.34
  615.7 3.0 convolution_convert_fusion.1
  618.8 5.7 reshape.499
  624.6 3.3 maximum_bitcast_fusion
  627.9 2.3 copy.125
  630.3 3.7 fusion.18
  634.0 5.9 convert_element_type.247
  642.6 3.1 collective-permute-start.20
  646.2 2.6 fusion.42
  648.8 3.9 collective-permute-done.19
  653.7 27.8 %reduce-scatter.12.cloned.1.call-done = bf16[160,1536]{1,0:T(8,128)(2,1)} async-done(((bf16[1280,1536]{1,0:T(8,128)(2,1)}), bf16[160,1536]{1,0:T(8,128)(2,1)}) %reduce-scatter.12.cloned.1.call-update) | async-done | bytes 491536 | tf_op jit(solution)/shard_map/reduce_scatter | solution.py:388
  684.0 2.3 collective-permute-start.17
  687.0 11.2 %all_gather.56 = bf16[256,1152]{1,0:T(8,128)(2,1)S(1)} all-gather(bf16[32,1152]{1,0:T(8,128)(2,1)S(1)} %fusion.83), channel_id=1, replica_groups=mesh['ctx'=8,'fsdp'=4] {'ctx'}, dimensions={0}, use_global_device_ids=true | all-gather | bytes 663552 | tf_op jit(solution)/shard_map/all_gather | solution.py:323
  700.3 12.3 %all-gather.2 = bf16[8,36,1536]{2,1,0:T(8,128)(2,1)S(1)} all-gather(bf16[1,36,1536]{2,1,0:T(8,128)(2,1)S(1)} %fusion.90), channel_id=1, replica_groups=mesh['ctx'=8,'fsdp'=4] {'ctx'}, dimensions={0}, use_global_device_ids=true | all-gather | bytes 995328 | tf_op jit(solution)/shard_map/all_gather | solution.py:391
  716.0 23.1 %all-gather.23.cloned.1.call-done = bf16[2304,1792]{1,0:T(8,128)(2,1)} async-done(((bf16[288,1792]{1,0:T(8,128)(2,1)}), bf16[2304,1792]{1,0:T(8,128)(2,1)}) %all-gather.23.cloned.1.call-update) | async-done | bytes 8257552 | tf_op jit(solution)/shard_map/all_gather | solution.py:398
  739.1 3.3 copy-done
  742.4 7.8 %shard_map.280 = (f32[288,6912]{1,0:T(8,128)}, f32[288,6912]{1,0:T(8,128)}) custom-call(bf16[8,288,1792]{2,1,0:T(8,128)(2,1)S(1)} %bitcast.231), custom_call_target="tpu_custom_call" | custom-call | tf_op jit(solution)/shard_map/pallas_call | solution.py:147
  (311 shorter events, 101.6 us)
Async XLA Ops:
  7.2 22.9 %copy-start.8 = (bf16[1,256,1152]{2,1,0:T(8,128)(2,1)S(1)}, bf16[1,256,1152]{2,1,0:T(8,128)(2,1)}, u32[]{:S(2)}) copy-start(bf16[1,256,1152]{2,1,0:T(8,128)(2,1)} %param.17) | copy-start | bytes 1769476
  7.2 57.6 %all-gather.21.cloned.1.call-start = ((), (), s32[]{:S(2)}) async-start(), calls=%async_computation.15 | async-start | bytes 4423680 | tf_op jit(solution)/shard_map/all_gather | solution.py:198
  12.5 9.3 %collective-permute-start = (bf16[37,1536]{1,0:T(8,128)(2,1)S(1)}, bf16[37,1536]{1,0:T(8,128)(2,1)S(1)}, u32[]{:S(2)}, u32[]{:S(2)}) collective-permute-start(bf16[37,1536]{1,0:T(8,128)(2,1)S(1)} %get-tuple-element.68), channel_id=1, source_target_pairs={{0,1},{1,2},{2,3},{3,0},{4,5},{5,6},{6,7},{7,4},{8,9},{9,10},{10,1... | collective-permute-start | bytes 341000 | tf_op jit(solution)/shard_map/ppermute | solution.py:79
  15.6 10.7 %collective-permute-start.1 = (bf16[37,1536]{1,0:T(8,128)(2,1)S(1)}, bf16[37,1536]{1,0:T(8,128)(2,1)S(1)}, u32[]{:S(2)}, u32[]{:S(2)}) collective-permute-start(bf16[37,1536]{1,0:T(8,128)(2,1)S(1)} %get-tuple-element.68), channel_id=1, source_target_pairs={{0,2},{1,3},{2,0},{3,1},{4,6},{5,7},{6,4},{7,5},{8,10},{9,11},{10,... | collective-permute-start | bytes 341000 | tf_op jit(solution)/shard_map/ppermute | solution.py:79
  18.2 8.1 %collective-permute-start.2 = (bf16[37,1536]{1,0:T(8,128)(2,1)S(1)}, bf16[37,1536]{1,0:T(8,128)(2,1)S(1)}, u32[]{:S(2)}, u32[]{:S(2)}) collective-permute-start(bf16[37,1536]{1,0:T(8,128)(2,1)S(1)} %get-tuple-element.68), channel_id=1, source_target_pairs={{0,3},{1,0},{2,1},{3,2},{4,7},{5,4},{6,5},{7,6},{8,11},{9,8},{10,9... | collective-permute-start | bytes 341000 | tf_op jit(solution)/shard_map/ppermute | solution.py:79
  27.2 122.6 %all-gather.11.cloned.1.call-start = ((), (), s32[]{:S(2)}) async-start(), calls=%async_computation.5 | async-start | bytes 2359296 | tf_op jit(solution)/shard_map/all_gather | solution.py:260
  28.7 54.6 %copy-start.62 = (f32[128]{0:T(128)}, f32[128]{0:T(128)S(1)}, u32[]{:S(2)}) copy-start(f32[128]{0:T(128)S(1)} %negate_power_fusion) | copy-start | bytes 1540
  30.1 53.2 %copy-start.51 = (f32[256]{0:T(256)}, f32[256]{0:T(256)S(1)}, u32[]{:S(2)}) copy-start(f32[256]{0:T(256)S(1)} %get-tuple-element.64) | copy-start | bytes 3076
  30.3 48.0 %copy-start.59 = (f32[256]{0:T(256)}, f32[256]{0:T(256)S(1)}, u32[]{:S(2)}) copy-start(f32[256]{0:T(256)S(1)} %fusion.94) | copy-start | bytes 3076
  31.4 50.3 %copy-start.38 = (f32[256]{0:T(256)}, f32[256]{0:T(256)S(1)}, u32[]{:S(2)}) copy-start(f32[256]{0:T(256)S(1)} %mul.591) | copy-start | bytes 3076
  31.5 46.8 %copy-start.36 = (f32[1152]{0:T(1024)}, f32[1152]{0:T(1024)S(1)}, u32[]{:S(2)}) copy-start(f32[1152]{0:T(1024)S(1)} %mul.568) | copy-start | bytes 13828
  83.8 25.4 %copy-start.24 = (f32[256,128]{1,0:T(8,128)}, f32[256,128]{1,0:T(8,128)S(1)}, u32[]{:S(2)}) copy-start(f32[256,128]{1,0:T(8,128)S(1)} %get-tuple-element.110) | copy-start | bytes 393220
  83.8 25.4 %copy-start.26 = (f32[256,128]{1,0:T(8,128)}, f32[256,128]{1,0:T(8,128)S(1)}, u32[]{:S(2)}) copy-start(f32[256,128]{1,0:T(8,128)S(1)} %get-tuple-element.111) | copy-start | bytes 393220
  84.6 85.6 %all-gather.13.cloned.1.call-start = ((), (), s32[]{:S(2)}) async-start(), calls=%async_computation.6 | async-start | bytes 2654208 | tf_op jit(solution)/shard_map/all_gather | solution.py:210
  85.6 6.8 collective-permute-start.5
  87.1 8.0 %collective-permute-start.6 = (bf16[32,1152]{1,0:T(8,128)(2,1)S(1)}, bf16[32,1152]{1,0:T(8,128)(2,1)S(1)}, u32[]{:S(2)}, u32[]{:S(2)}) collective-permute-start(bf16[32,1152]{1,0:T(8,128)(2,1)S(1)} %get-tuple-element.63), channel_id=1, source_target_pairs={{0,2},{1,3},{2,0},{3,1},{4,6},{5,7},{6,4},{7,5},{8,10},{9,11},{10,... | collective-permute-start | bytes 221192 | tf_op jit(solution)/shard_map/ppermute | solution.py:79
  89.6 5.8 collective-permute-start.7
  96.1 151.6 %all-gather.15.cloned.1.call-start = ((), (), s32[]{:S(2)}) async-start(), calls=%async_computation.7 | async-start | bytes 5308416 | tf_op jit(solution)/shard_map/all_gather | solution.py:282
  100.2 69.9 %collective-permute-start.4 = (bf16[288,1792]{1,0:T(8,128)(2,1)}, bf16[288,1792]{1,0:T(8,128)(2,1)}, u32[]{:S(2)}, u32[]{:S(2)}) collective-permute-start(bf16[288,1792]{1,0:T(8,128)(2,1)} %concatenate.42), channel_id=1, source_target_pairs={{0,2},{1,3},{2,0},{3,1},{4,6},{5,7},{6,4},{7,5},{8,10},{9,11},{10,... | collective-permute-start | bytes 3096584 | tf_op jit(solution)/shard_map/ppermute | solution.py:79
  101.1 48.7 %collective-permute-start.3 = (bf16[288,1792]{1,0:T(8,128)(2,1)}, bf16[288,1792]{1,0:T(8,128)(2,1)}, u32[]{:S(2)}, u32[]{:S(2)}) collective-permute-start(bf16[288,1792]{1,0:T(8,128)(2,1)} %concatenate.42), channel_id=1, source_target_pairs={{0,1},{1,2},{2,3},{3,0},{4,5},{5,6},{6,7},{7,4},{8,9},{9,10},{10,1... | collective-permute-start | bytes 3096584 | tf_op jit(solution)/shard_map/ppermute | solution.py:79
  104.3 48.8 %copy-start.11 = (pred[256,2048]{1,0:T(8,128)(4,1)}, pred[256,2048]{1,0:T(8,128)(4,1)S(1)}, u32[]{:S(2)}) copy-start(pred[256,2048]{1,0:T(8,128)(4,1)S(1)} %compare_and_fusion) | copy-start | bytes 1572868
  109.7 43.4 %copy-start.20 = (bf16[256,4,256]{2,0,1:T(8,128)(2,1)}, bf16[256,4,256]{2,0,1:T(8,128)(2,1)S(1)}, u32[]{:S(2)}) copy-start(bf16[256,4,256]{2,0,1:T(8,128)(2,1)S(1)} %fusion.48) | copy-start | bytes 1572868
  158.7 14.1 %copy-start.22 = (bf16[4,256,256]{1,2,0:T(8,128)(2,1)}, bf16[4,256,256]{1,2,0:T(8,128)(2,1)S(1)}, u32[]{:S(2)}) copy-start(bf16[4,256,256]{1,2,0:T(8,128)(2,1)S(1)} %convolution_convert_fusion.7) | copy-start | bytes 1572868
  173.4 295.5 %copy-start.49 = (f32[256]{0:T(256)}, f32[256]{0:T(256)S(1)}, u32[]{:S(2)}) copy-start(f32[256]{0:T(256)S(1)} %fusion.97) | copy-start | bytes 3076
  174.4 162.9 %reduce-scatter.6.cloned.1.call-start = ((), (), s32[]{:S(2)}) async-start(), calls=%async_computation.8 | async-start | bytes 5308416 | tf_op jit(solution)/shard_map/reduce_scatter | solution.py:291
  174.4 72.2 %collective-permute-start.8 = (bf16[288,1792]{1,0:T(8,128)(2,1)}, bf16[288,1792]{1,0:T(8,128)(2,1)S(1)}, u32[]{:S(2)}, u32[]{:S(2)}) collective-permute-start(bf16[288,1792]{1,0:T(8,128)(2,1)} %concatenate.42), channel_id=1, source_target_pairs={{0,3},{1,0},{2,1},{3,2},{4,7},{5,4},{6,5},{7,6},{8,11},{9,8},{10,9... | collective-permute-start | bytes 3096584 | tf_op jit(solution)/shard_map/ppermute | solution.py:79
  177.9 62.7 %collective-permute-start.10 = (bf16[216,1152]{1,0:T(8,128)(2,1)S(1)}, bf16[216,1152]{1,0:T(8,128)(2,1)S(1)}, u32[]{:S(2)}, u32[]{:S(2)}) collective-permute-start(bf16[216,1152]{1,0:T(8,128)(2,1)S(1)} %get-tuple-element.59), channel_id=1, source_target_pairs={{0,2},{1,3},{2,0},{3,1},{4,6},{5,7},{6,4},{7,5},{8,10},{9,11},{10,... | collective-permute-start | bytes 1493000 | tf_op jit(solution)/shard_map/ppermute | solution.py:79
  188.1 43.3 %collective-permute-start.9 = (bf16[216,1152]{1,0:T(8,128)(2,1)S(1)}, bf16[216,1152]{1,0:T(8,128)(2,1)S(1)}, u32[]{:S(2)}, u32[]{:S(2)}) collective-permute-start(bf16[216,1152]{1,0:T(8,128)(2,1)S(1)} %get-tuple-element.59), channel_id=1, source_target_pairs={{0,1},{1,2},{2,3},{3,0},{4,5},{5,6},{6,7},{7,4},{8,9},{9,10},{10,1... | collective-permute-start | bytes 1493000 | tf_op jit(solution)/shard_map/ppermute | solution.py:79
  190.1 51.3 %collective-permute-start.11 = (bf16[216,1152]{1,0:T(8,128)(2,1)S(1)}, bf16[216,1152]{1,0:T(8,128)(2,1)S(1)}, u32[]{:S(2)}, u32[]{:S(2)}) collective-permute-start(bf16[216,1152]{1,0:T(8,128)(2,1)S(1)} %get-tuple-element.59), channel_id=1, source_target_pairs={{0,3},{1,0},{2,1},{3,2},{4,7},{5,4},{6,5},{7,6},{8,11},{9,8},{10,9... | collective-permute-start | bytes 1493000 | tf_op jit(solution)/shard_map/ppermute | solution.py:79
  276.8 61.8 %copy-start.10 = (bf16[1,256,1152]{2,1,0:T(8,128)(2,1)S(1)}, bf16[1,256,1152]{2,1,0:T(8,128)(2,1)}, u32[]{:S(2)}) copy-start(bf16[1,256,1152]{2,1,0:T(8,128)(2,1)} %param.20) | copy-start | bytes 1769476
  276.8 105.3 %all-gather.17.cloned.1.call-start = ((), (), s32[]{:S(2)}) async-start(), calls=%async_computation.9 | async-start | bytes 5308416 | tf_op jit(solution)/shard_map/all_gather | solution.py:298
  276.9 120.2 %copy-start.31 = (f32[1152]{0:T(1024)}, f32[1152]{0:T(1024)S(1)}, u32[]{:S(2)}) copy-start(f32[1152]{0:T(1024)S(1)} %mul.621) | copy-start | bytes 13828
  338.6 58.6 %copy-start.50 = (f32[256]{0:T(256)}, f32[256]{0:T(256)S(1)}, u32[]{:S(2)}) copy-start(f32[256]{0:T(256)S(1)} %fusion.98) | copy-start | bytes 3076
  343.0 124.7 %reduce-scatter.8.cloned.1.call-start = ((), (), s32[]{:S(2)}) async-start(), calls=%async_computation.10 | async-start | bytes 5308416 | tf_op jit(solution)/shard_map/reduce_scatter | solution.py:303
  413.7 142.4 %reduce-scatter.10.cloned.1.call-start = ((), (), s32[]{:S(2)}) async-start(), calls=%async_computation.11 | async-start | bytes 2359296 | tf_op jit(solution)/shard_map/reduce_scatter | solution.py:336
  414.5 10.0 %copy-start.67 = (bf16[2048,896]{0,1:T(8,128)(2,1)S(1)}, bf16[2048,896]{0,1:T(8,128)(2,1)}, u32[]{:S(2)}) copy-start(bf16[2048,896]{0,1:T(8,128)(2,1)} %copy-done.66) | copy-start | bytes 11010052
  442.0 49.7 %collective-permute-start.12 = (bf16[288,1792]{1,0:T(8,128)(2,1)}, bf16[288,1792]{1,0:T(8,128)(2,1)}, u32[]{:S(2)}, u32[]{:S(2)}) collective-permute-start(bf16[288,1792]{1,0:T(8,128)(2,1)} %get-tuple-element.73), channel_id=1, source_target_pairs={{0,1},{1,2},{2,3},{3,0},{4,5},{5,6},{6,7},{7,4},{8,9},{9,10},{10,1... | collective-permute-start | bytes 3096584 | tf_op jit(solution)/shard_map/ppermute | solution.py:79
  491.7 49.1 %copy-start.46 = (bf16[1152]{0:T(1024)(128)(2,1)S(1)}, bf16[1152]{0:T(1024)(128)(2,1)}, u32[]{:S(2)}) copy-start(bf16[1152]{0:T(1024)(128)(2,1)} %get-tuple-element.51) | copy-start | bytes 6916
  491.7 142.3 %all-gather.19.cloned.1.call-start = ((), (), s32[]{:S(2)}) async-start(), calls=%async_computation.14 | async-start | bytes 4478976 | tf_op jit(solution)/shard_map/all_gather | solution.py:396
  492.6 16.1 %collective-permute-start.21 = (bf16[216,1152]{1,0:T(8,128)(2,1)S(1)}, bf16[216,1152]{1,0:T(8,128)(2,1)S(1)}, u32[]{:S(2)}, u32[]{:S(2)}) collective-permute-start(bf16[216,1152]{1,0:T(8,128)(2,1)S(1)} %get-tuple-element.82), channel_id=1, source_target_pairs={{0,1},{1,2},{2,3},{3,0},{4,5},{5,6},{6,7},{7,4},{8,9},{9,10},{10,1... | collective-permute-start | bytes 1493000 | tf_op jit(solution)/shard_map/ppermute | solution.py:79
  494.2 23.5 %collective-permute-start.23 = (bf16[216,1152]{1,0:T(8,128)(2,1)S(1)}, bf16[216,1152]{1,0:T(8,128)(2,1)S(1)}, u32[]{:S(2)}, u32[]{:S(2)}) collective-permute-start(bf16[216,1152]{1,0:T(8,128)(2,1)S(1)} %get-tuple-element.83), channel_id=1, source_target_pairs={{0,3},{1,0},{2,1},{3,2},{4,7},{5,4},{6,5},{7,6},{8,11},{9,8},{10,9... | collective-permute-start | bytes 1493000 | tf_op jit(solution)/shard_map/ppermute | solution.py:79
  496.5 43.1 %collective-permute-start.22 = (bf16[216,1152]{1,0:T(8,128)(2,1)S(1)}, bf16[216,1152]{1,0:T(8,128)(2,1)S(1)}, u32[]{:S(2)}, u32[]{:S(2)}) collective-permute-start(bf16[216,1152]{1,0:T(8,128)(2,1)S(1)} %get-tuple-element.84), channel_id=1, source_target_pairs={{0,2},{1,3},{2,0},{3,1},{4,6},{5,7},{6,4},{7,5},{8,10},{9,11},{10,... | collective-permute-start | bytes 1493000 | tf_op jit(solution)/shard_map/ppermute | solution.py:79
  540.6 99.3 %reduce-scatter.14.cloned.1.call-start = ((), (), s32[]{:S(2)}) async-start(), calls=%async_computation.13 | async-start | bytes 2654208 | tf_op jit(solution)/shard_map/reduce_scatter | solution.py:321
  540.9 89.4 %collective-permute-start.14 = (bf16[288,1792]{1,0:T(8,128)(2,1)}, bf16[288,1792]{1,0:T(8,128)(2,1)}, u32[]{:S(2)}, u32[]{:S(2)}) collective-permute-start(bf16[288,1792]{1,0:T(8,128)(2,1)} %get-tuple-element.71), channel_id=1, source_target_pairs={{0,3},{1,0},{2,1},{3,2},{4,7},{5,4},{6,5},{7,6},{8,11},{9,8},{10,9... | collective-permute-start | bytes 3096584 | tf_op jit(solution)/shard_map/ppermute | solution.py:79
  542.4 65.6 %collective-permute-start.13 = (bf16[288,1792]{1,0:T(8,128)(2,1)}, bf16[288,1792]{1,0:T(8,128)(2,1)}, u32[]{:S(2)}, u32[]{:S(2)}) collective-permute-start(bf16[288,1792]{1,0:T(8,128)(2,1)} %get-tuple-element.72), channel_id=1, source_target_pairs={{0,2},{1,3},{2,0},{3,1},{4,6},{5,7},{6,4},{7,5},{8,10},{9,11},{10,... | collective-permute-start | bytes 3096584 | tf_op jit(solution)/shard_map/ppermute | solution.py:79
  546.1 6.9 copy-start.5
  546.1 6.9 copy-start.33
  546.1 6.9 copy-start.41
  546.2 135.3 %reduce-scatter.12.cloned.1.call-start = ((), (), s32[]{:S(2)}) async-start(), calls=%async_computation.12 | async-start | bytes 4423680 | tf_op jit(solution)/shard_map/reduce_scatter | solution.py:388
  553.0 55.1 %copy-start.52 = (f32[256]{0:T(256)S(1)}, f32[256]{0:T(256)}, u32[]{:S(2)}) copy-start(f32[256]{0:T(256)} %copy-done.51) | copy-start | bytes 3076
  553.0 55.1 %copy-start.63 = (f32[128]{0:T(128)S(1)}, f32[128]{0:T(128)}, u32[]{:S(2)}) copy-start(f32[128]{0:T(128)} %copy-done.62) | copy-start | bytes 1540
  553.0 55.6 %copy-start.39 = (f32[256]{0:T(256)S(1)}, f32[256]{0:T(256)}, u32[]{:S(2)}) copy-start(f32[256]{0:T(256)} %copy-done.38) | copy-start | bytes 3076
  553.0 55.6 %copy-start.43 = (f32[256]{0:T(256)S(1)}, f32[256]{0:T(256)}, u32[]{:S(2)}) copy-start(f32[256]{0:T(256)} %copy-done.42) | copy-start | bytes 3076
  553.5 56.3 %copy-start.56 = (f32[256]{0:T(256)S(1)}, f32[256]{0:T(256)}, u32[]{:S(2)}) copy-start(f32[256]{0:T(256)} %copy-done.55) | copy-start | bytes 3076
  553.5 57.6 %copy-start.9 = (bf16[1,256,1152]{2,1,0:T(8,128)(2,1)S(1)}, bf16[1,256,1152]{2,1,0:T(8,128)(2,1)}, u32[]{:S(2)}) copy-start(bf16[1,256,1152]{2,1,0:T(8,128)(2,1)} %param.17) | copy-start | bytes 1769476
  553.5 57.6 %copy-start.37 = (f32[1152]{0:T(1024)S(1)}, f32[1152]{0:T(1024)}, u32[]{:S(2)}) copy-start(f32[1152]{0:T(1024)} %copy-done.36) | copy-start | bytes 13828
  553.5 57.6 %copy-start.60 = (f32[256]{0:T(256)S(1)}, f32[256]{0:T(256)}, u32[]{:S(2)}) copy-start(f32[256]{0:T(256)} %copy-done.59) | copy-start | bytes 3076
  630.3 108.8 %all-gather.23.cloned.1.call-start = ((), (), s32[]{:S(2)}) async-start(), calls=%async_computation.16 | async-start | bytes 9289728 | tf_op jit(solution)/shard_map/all_gather | solution.py:398
  641.0 7.8 %collective-permute-start.18 = (bf16[32,1152]{1,0:T(8,128)(2,1)S(1)}, bf16[32,1152]{1,0:T(8,128)(2,1)S(1)}, u32[]{:S(2)}, u32[]{:S(2)}) collective-permute-start(bf16[32,1152]{1,0:T(8,128)(2,1)S(1)} %get-tuple-element.97), channel_id=1, source_target_pairs={{0,1},{1,2},{2,3},{3,0},{4,5},{5,6},{6,7},{7,4},{8,9},{9,10},{10,1... | collective-permute-start | bytes 221192 | tf_op jit(solution)/shard_map/ppermute | solution.py:79
  642.6 6.2 collective-permute-start.20
  645.7 7.0 collective-permute-start.19
  682.5 16.8 %collective-permute-start.15 = (bf16[37,1536]{1,0:T(8,128)(2,1)S(1)}, bf16[37,1536]{1,0:T(8,128)(2,1)S(1)}, u32[]{:S(2)}, u32[]{:S(2)}) collective-permute-start(bf16[37,1536]{1,0:T(8,128)(2,1)S(1)} %get-tuple-element.94), channel_id=1, source_target_pairs={{0,1},{1,2},{2,3},{3,0},{4,5},{5,6},{6,7},{7,4},{8,9},{9,10},{10,1... | collective-permute-start | bytes 341000 | tf_op jit(solution)/shard_map/ppermute | solution.py:79
  684.0 15.3 %collective-permute-start.17 = (bf16[37,1536]{1,0:T(8,128)(2,1)S(1)}, bf16[37,1536]{1,0:T(8,128)(2,1)S(1)}, u32[]{:S(2)}, u32[]{:S(2)}) collective-permute-start(bf16[37,1536]{1,0:T(8,128)(2,1)S(1)} %get-tuple-element.95), channel_id=1, source_target_pairs={{0,3},{1,0},{2,1},{3,2},{4,7},{5,4},{6,5},{7,6},{8,11},{9,8},{10,9... | collective-permute-start | bytes 341000 | tf_op jit(solution)/shard_map/ppermute | solution.py:79
  686.4 13.0 %collective-permute-start.16 = (bf16[37,1536]{1,0:T(8,128)(2,1)S(1)}, bf16[37,1536]{1,0:T(8,128)(2,1)S(1)}, u32[]{:S(2)}, u32[]{:S(2)}) collective-permute-start(bf16[37,1536]{1,0:T(8,128)(2,1)S(1)} %get-tuple-element.96), channel_id=1, source_target_pairs={{0,2},{1,3},{2,0},{3,1},{4,6},{5,7},{6,4},{7,5},{8,10},{9,11},{10,... | collective-permute-start | bytes 341000 | tf_op jit(solution)/shard_map/ppermute | solution.py:79
  (40 other events, 113.4 us)
Sparse Core Ops, SparseCore 0:
  27.3 37.4 all-gather.20
  84.7 27.8 all-gather.10
  115.1 29.0 all-gather.12
  174.5 45.7 all-gather.14
  276.9 60.3 reduce-scatter.5
  343.1 38.8 all-gather.16
  413.8 53.9 reduce-scatter.7
  491.8 41.1 reduce-scatter.9
  540.8 33.9 all-gather.18
  578.3 42.5 reduce-scatter.13
  630.4 51.0 reduce-scatter.11
  683.4 55.6 all-gather.22
